TPU v7x, 32 devices: a whole 2x2x4 slice. The times are simulated.
32 devices in a mesh: dp: 2 (over y), ulysses: 8 (over z, core), blk: 2 (over x).
Axes of the slice: x: 2, y: 2, z: 4, core: 2. Of those that a mesh axis runs over, the one named last changes fastest.
Arguments:
- tokens: bfloat16 [4, 1024, 1024], P('dp', ('ulysses', 'blk')), may hold values from -6 to 6
- norm_gain_attn: bfloat16 [1024], P(('dp', 'ulysses', 'blk')), may hold values from 0.5 to 1.5
- query_key_value_weight: bfloat16 [1024, 3072], P(('dp', 'ulysses', 'blk')), may hold values from -0.1875 to 0.1875
- attention_output_weight: bfloat16 [1024, 1024], P(('dp', 'ulysses', 'blk')), may hold values from -2 to 2
- norm_gain_mlp: bfloat16 [1024], P(('dp', 'ulysses', 'blk')), may hold values from 0.5 to 1.5
- input_projection_weight: bfloat16 [1024, 5248], P(('dp', 'ulysses', 'blk')), may hold values from -0.1875 to 0.1875
- down_projection_weight: bfloat16 [1024, 2624], P(('dp', 'ulysses', 'blk')), may hold values from -0.125 to 0.125
- cotangent: bfloat16 [4, 1024, 1024], P('dp', ('ulysses', 'blk')), may hold values from -6 to 6
Outputs:
- output: bfloat16 [4, 1024, 1024], P('dp', ('ulysses', 'blk'))
- input_grad: float32 [4, 1024, 1024], P('dp', ('ulysses', 'blk'))
- grad_norm_gain_attn: float32 [1024], P(('dp', 'ulysses', 'blk'))
- grad_qkv_weight: float32 [1024, 3072], P(('dp', 'ulysses', 'blk'))
- grad_out_weight: float32 [1024, 1024], P(('dp', 'ulysses', 'blk'))
- grad_norm_gain_mlp: float32 [1024], P(('dp', 'ulysses', 'blk'))
- grad_in_weight: float32 [1024, 5248], P(('dp', 'ulysses', 'blk'))
- grad_down_weight: float32 [1024, 2624], P(('dp', 'ulysses', 'blk'))
All inputs are finite; a program needn't handle non-finite values.
Results may differ from a plain program's by a relative error of at most 0.023.
Values may be sent and summed in bfloat16 or wider, within the bound.
A program may use at most 256 MiB of HBM per device.

v0:
```python
import math

import jax
import jax.numpy as jnp
from jax import lax
from jax.sharding import PartitionSpec as P

FF = 2624
HEADS = 16
HEAD_DIM = 64


EPSILON = 1e-05
ROPE_BASE = 160000.0


def as_sent(shard):

    def short(part):
        return part.astype(jnp.bfloat16) if part.dtype == jnp.float32 else part

    return jax.tree.map(short, shard)


def layer_norm(values, gain):
    average = jnp.mean(values, axis=-1, keepdims=True)
    centered = values - average
    variance = jnp.mean(centered * centered, axis=-1, keepdims=True)
    return centered * lax.rsqrt(variance + EPSILON) * gain


def rope_tables(positions, half_dim):
    ladder = jnp.arange(half_dim, dtype=jnp.float32)
    frequency = ROPE_BASE ** (-2.0 * ladder / (2 * half_dim))
    angles = positions[:, None] * frequency[None, :]
    return (jnp.cos(angles)[:, None, :], jnp.sin(angles)[:, None, :])


def rotate(values, cosine, sine):
    half_dim = values.shape[-1] // 2
    first_half = values[..., :half_dim]
    second_half = values[..., half_dim:]
    return jnp.concatenate(
        [first_half * cosine - second_half * sine, second_half * cosine + first_half * sine],
        axis=-1,
    )


def rotate_back(gradient, cosine, sine):
    half_dim = gradient.shape[-1] // 2
    first_half = gradient[..., :half_dim]
    second_half = gradient[..., half_dim:]
    return jnp.concatenate(
        [first_half * cosine + second_half * sine, second_half * cosine - first_half * sine],
        axis=-1,
    )


def gated_unit(hidden_input):
    return jax.nn.gelu(hidden_input[:, :FF], approximate=False) * hidden_input[:, FF:]


def contract_rows(left_side, right_side):
    return lax.dot_general(
        left_side, right_side, (((0,), (0,)), ((), ())), preferred_element_type=jnp.float32
    )


def contract_cols(left_side, right_side):
    return lax.dot_general(
        left_side, right_side, (((1,), (1,)), ((), ())), preferred_element_type=jnp.float32
    )


def stack_front(pieces):
    return tuple((piece.reshape((1,) + piece.shape) for piece in pieces))


def add_front(received):
    return tuple((jnp.sum(piece, axis=0) for piece in received))


def attend_block(query_block, keys_seq, values_seq):
    scale_factor = 1.0 / math.sqrt(query_block.shape[-1])
    scores = (
        jnp.einsum("bhe,khe->hbk", query_block, keys_seq, preferred_element_type=jnp.float32)
        * scale_factor
    )
    row_peak = jnp.max(scores, axis=-1, keepdims=True)
    exponent = jnp.exp(scores - row_peak)
    total = jnp.sum(exponent, axis=-1, keepdims=True)
    weights_low = (exponent / total).astype(jnp.bfloat16)
    result = jnp.einsum("hbk,khe->bhe", weights_low, values_seq, preferred_element_type=jnp.float32)
    return (result.astype(jnp.bfloat16), (row_peak + jnp.log(total))[..., 0])


def attend_sequence(queries_seq, keys_seq, values_seq, block):
    count = queries_seq.shape[0] // block
    query_blocks = queries_seq.reshape((count, block) + queries_seq.shape[1:])
    results, log_totals = lax.map(
        lambda query_block: attend_block(query_block, keys_seq, values_seq), query_blocks
    )
    return (results.reshape(queries_seq.shape), log_totals)


def grad_sequence(queries_seq, keys_seq, values_seq, log_totals, grad_seq, block):
    count = queries_seq.shape[0] // block
    scale_factor = 1.0 / math.sqrt(queries_seq.shape[-1])
    query_blocks = queries_seq.reshape((count, block) + queries_seq.shape[1:])
    grad_blocks = grad_seq.reshape((count, block) + grad_seq.shape[1:])

    def one_block(carry, items):
        key_grad, value_grad = carry
        query_block, grad_block, log_block = items
        scores = (
            jnp.einsum("bhe,khe->hbk", query_block, keys_seq, preferred_element_type=jnp.float32)
            * scale_factor
        )
        weights = jnp.exp(scores - log_block[..., None])
        grad_weights = jnp.einsum(
            "bhe,khe->hbk", grad_block, values_seq, preferred_element_type=jnp.float32
        )
        inner_sum = jnp.sum(weights * grad_weights, axis=-1, keepdims=True)
        grad_scores = (weights * (grad_weights - inner_sum)).astype(jnp.bfloat16)
        query_grad = (
            jnp.einsum("hbk,khe->bhe", grad_scores, keys_seq, preferred_element_type=jnp.float32)
            * scale_factor
        )
        key_grad = (
            key_grad
            + jnp.einsum(
                "hbk,bhe->khe", grad_scores, query_block, preferred_element_type=jnp.float32
            )
            * scale_factor
        )
        value_grad = value_grad + jnp.einsum(
            "hbk,bhe->khe",
            weights.astype(jnp.bfloat16),
            grad_block,
            preferred_element_type=jnp.float32,
        )
        return ((key_grad, value_grad), query_grad)

    zero_keys = jnp.zeros(keys_seq.shape, jnp.float32)
    (key_grad, value_grad), query_grads = lax.scan(
        one_block, (zero_keys, zero_keys), (query_blocks, grad_blocks, log_totals)
    )
    return (query_grads.reshape(queries_seq.shape), key_grad, value_grad)


def body(
    tokens,
    norm_gain_attn,
    query_key_value_weight,
    attention_output_weight,
    norm_gain_mlp,
    input_projection_weight,
    down_projection_weight,
    cotangent,
):
    seq_count, local_len, width = tokens.shape
    gain_attn, qkv_full, out_full, gain_mlp, in_full, down_full = (
        lax.all_gather(norm_gain_attn, ("dp", "ulysses", "blk"), axis=0, tiled=True),
        lax.all_gather(query_key_value_weight, ("dp", "ulysses", "blk"), axis=0, tiled=True),
        lax.all_gather(attention_output_weight, ("dp", "ulysses", "blk"), axis=0, tiled=True),
        lax.all_gather(norm_gain_mlp, ("dp", "ulysses", "blk"), axis=0, tiled=True),
        lax.all_gather(input_projection_weight, ("dp", "ulysses", "blk"), axis=0, tiled=True),
        lax.all_gather(down_projection_weight, ("dp", "ulysses", "blk"), axis=0, tiled=True),
    )
    inputs = tokens.astype(jnp.float32).reshape(-1, width)
    gain_attn_f = gain_attn.astype(jnp.float32)
    normed_attention_input = layer_norm(inputs, gain_attn_f).astype(jnp.bfloat16)
    joined_heads = jnp.dot(
        normed_attention_input, qkv_full, preferred_element_type=jnp.float32
    ).astype(jnp.bfloat16)
    joined_heads = joined_heads.reshape(seq_count, local_len, HEADS, 3 * HEAD_DIM)
    heads = lax.all_to_all(joined_heads, "ulysses", split_axis=2, concat_axis=1, tiled=True)
    cycle_size = lax.axis_size("blk")
    cycle_index = lax.axis_index("blk")
    row_ids = jnp.arange(heads.shape[1], dtype=jnp.int32)
    positions = (row_ids // local_len * cycle_size + cycle_index) * local_len + row_ids % local_len
    cosine, sine = rope_tables(positions.astype(jnp.float32), HEAD_DIM // 2)
    queries = rotate(heads[..., :HEAD_DIM].astype(jnp.float32), cosine, sine).astype(jnp.bfloat16)
    keys_local = rotate(
        heads[..., HEAD_DIM : 2 * HEAD_DIM].astype(jnp.float32), cosine, sine
    ).astype(jnp.bfloat16)
    values_local = heads[..., 2 * HEAD_DIM :]
    keys_all, values_all = (
        lax.all_gather(keys_local, "blk", axis=1, tiled=True),
        lax.all_gather(values_local, "blk", axis=1, tiled=True),
    )
    block = min(512, heads.shape[1])
    attended_list = []
    log_list = []
    for seq_index in range(seq_count):
        result, log_totals = attend_sequence(
            queries[seq_index], keys_all[seq_index], values_all[seq_index], block
        )
        attended_list.append(result)
        log_list.append(log_totals)
    attended_rows = jnp.stack(attended_list)
    gathered_back = lax.all_to_all(
        attended_rows, "ulysses", split_axis=1, concat_axis=2, tiled=True
    ).reshape(-1, width)
    middle_hidden = inputs + jnp.dot(gathered_back, out_full, preferred_element_type=jnp.float32)
    gain_mlp_f = gain_mlp.astype(jnp.float32)
    normed_feedforward_input = layer_norm(middle_hidden, gain_mlp_f).astype(jnp.bfloat16)
    hidden_input = jnp.dot(normed_feedforward_input, in_full, preferred_element_type=jnp.float32)
    activated_half = gated_unit(hidden_input).astype(jnp.bfloat16)
    mlp_result = contract_cols(activated_half, down_full)
    output = (middle_hidden + mlp_result).astype(jnp.bfloat16).reshape(tokens.shape)
    grad_top = cotangent.reshape(-1, width)
    grad_down = contract_rows(grad_top, activated_half)
    grad_active = jnp.dot(grad_top, down_full, preferred_element_type=jnp.float32)
    _, gated_pull = jax.vjp(gated_unit, hidden_input)
    grad_hidden = gated_pull(grad_active)[0].astype(jnp.bfloat16)
    grad_in = contract_rows(normed_feedforward_input, grad_hidden)
    grad_normed_mlp = contract_cols(grad_hidden, in_full)
    _, norm_pull = jax.vjp(layer_norm, middle_hidden, gain_mlp_f)
    grad_middle_norm, grad_gain_mlp = norm_pull(grad_normed_mlp)
    grad_middle = grad_top.astype(jnp.float32) + grad_middle_norm
    grad_branch = grad_middle.astype(jnp.bfloat16)
    grad_out = contract_rows(gathered_back, grad_branch)
    grad_back = contract_cols(grad_branch, out_full).astype(jnp.bfloat16)
    grad_back = grad_back.reshape(seq_count, local_len, HEADS, HEAD_DIM)
    grad_heads = lax.all_to_all(grad_back, "ulysses", split_axis=2, concat_axis=1, tiled=True)
    query_list = []
    key_list = []
    value_list = []
    for seq_index in range(seq_count):
        query_grad, key_grad, value_grad = grad_sequence(
            queries[seq_index],
            keys_all[seq_index],
            values_all[seq_index],
            log_list[seq_index],
            grad_heads[seq_index],
            block,
        )
        query_list.append(query_grad)
        key_list.append(key_grad)
        value_list.append(value_grad)
    key_grads, value_grads = (
        lax.psum_scatter(
            jnp.stack(key_list).astype(jnp.bfloat16), "blk", scatter_dimension=1, tiled=True
        ).astype(jnp.float32),
        lax.psum_scatter(
            jnp.stack(value_list).astype(jnp.bfloat16), "blk", scatter_dimension=1, tiled=True
        ).astype(jnp.float32),
    )
    grad_joined = jnp.concatenate(
        [
            rotate_back(jnp.stack(query_list), cosine, sine),
            rotate_back(key_grads, cosine, sine),
            value_grads,
        ],
        axis=-1,
    ).astype(jnp.bfloat16)
    grad_tokens = lax.all_to_all(
        grad_joined, "ulysses", split_axis=1, concat_axis=2, tiled=True
    ).reshape(-1, 3 * width)
    grad_qkv = contract_rows(normed_attention_input, grad_tokens)
    grad_normed_attn = contract_cols(grad_tokens, qkv_full)
    _, first_pull = jax.vjp(layer_norm, inputs, gain_attn_f)
    grad_input_norm, grad_gain_attn = first_pull(grad_normed_attn)
    input_grad = (grad_middle + grad_input_norm).reshape(tokens.shape)
    every_rows = lax.all_to_all(
        as_sent(
            stack_front((grad_gain_attn, grad_qkv, grad_out, grad_gain_mlp, grad_in, grad_down))
        ),
        "dp",
        split_axis=1,
        concat_axis=0,
        tiled=True,
    )
    summed = tuple(
        jax.tree.map(
            lambda part: part.astype(jnp.float32),
            lax.psum_scatter(
                as_sent(add_front(every_rows)), ("ulysses", "blk"), scatter_dimension=0, tiled=True
            ),
        )
    )
    return (output, input_grad) + summed


def solution(mesh):
    in_specs = (
        P("dp", ("ulysses", "blk"), None),
        P(("dp", "ulysses", "blk")),
        P(("dp", "ulysses", "blk"), None),
        P(("dp", "ulysses", "blk"), None),
        P(("dp", "ulysses", "blk")),
        P(("dp", "ulysses", "blk"), None),
        P(("dp", "ulysses", "blk"), None),
        P("dp", ("ulysses", "blk"), None),
    )
    out_specs = (
        P("dp", ("ulysses", "blk"), None),
        P("dp", ("ulysses", "blk"), None),
        P(("dp", "ulysses", "blk")),
        P(("dp", "ulysses", "blk"), None),
        P(("dp", "ulysses", "blk"), None),
        P(("dp", "ulysses", "blk")),
        P(("dp", "ulysses", "blk"), None),
        P(("dp", "ulysses", "blk"), None),
    )
    return jax.shard_map(body, mesh=mesh, in_specs=in_specs, out_specs=out_specs, check_vma=False)
```

profile of v0, /device:TPU:0, one launch (start us, length us, event | category | flops | bytes accessed | tf_op | source)
XLA Modules:
  0.0 1024.5 jit_solution(16969515317121492687)
XLA Ops:
  11.7 42.5 %all-reduce.6 = (bf16[1024]{0:T(1024)(128)(2,1)S(1)}, bf16[1024]{0:T(1024)(128)(2,1)S(1)}) all-reduce(bf16[1024]{0:T(1024)(128)(2,1)S(1)} %dynamic-update-slice, bf16[1024]{0:T(1024)(128)(2,1)S(1)} %dynamic-update-slice.1), channel_id=1, replica_groups=mesh['dp'=2,'ulysses'=8,'blk'=2] {'dp','ulysses','blk'}, use_global_device_ids=true, to_apply=%add.2 | all-reduce | flops 2048 | bytes 8192
  58.9 24.4 %all-gather.5.cloned.1.call-done = bf16[1024,3072]{1,0:T(8,128)(2,1)} async-done(((bf16[32,3072]{1,0:T(8,128)(2,1)}), bf16[1024,3072]{1,0:T(8,128)(2,1)}) %all-gather.5.cloned.1.call-update) | async-done | bytes 6291472 | tf_op jit(solution)/shard_map/all_gather | solution.py:164
  83.2 3.8 convolution_convert_fusion.2
  89.5 3.6 all-to-all-start
  93.4 30.0 %all-to-all-done = bf16[2,64,16,192]{3,1,0,2:T(8,128)(2,1)S(1)} async-done(((bf16[2,64,16,192]{3,1,0,2:T(8,128)(2,1)}), bf16[2,64,16,192]{3,1,0,2:T(8,128)(2,1)S(1)}, u32[]{:S(2)}, u32[]{:S(2)}) %all-to-all-start) | async-done | bytes 786464 | tf_op jit(solution)/shard_map/all_to_all | solution.py:177
  124.7 12.1 %all_gather.27 = bf16[2,1024,2,64]{1,3,2,0:T(8,128)(2,1)S(1)} all-gather(bf16[2,512,2,64]{1,3,2,0:T(8,128)(2,1)S(1)} %pad_maximum_fusion.3), channel_id=1, replica_groups=mesh['dp'=2,'ulysses'=8,'blk'=2] {'blk'}, dimensions={1}, use_global_device_ids=true | all-gather | bytes 786432 | tf_op jit(solution)/shard_map/all_gather | solution.py:189
  136.8 7.0 all_gather.26
  151.3 3.9 all-to-all-start.1
  155.2 15.3 %all-to-all-done.1 = bf16[8,2,8192]{2,1,0:T(2,128)(2,1)S(1)} async-done(((bf16[8,2,8192]{2,1,0:T(2,128)(2,1)}), bf16[8,2,8192]{2,1,0:T(2,128)(2,1)S(1)}, u32[]{:S(2)}, u32[]{:S(2)}) %all-to-all-start.1) | async-done | bytes 262176 | tf_op jit(solution)/shard_map/all_to_all | solution.py:202
  171.7 2.2 fusion.93
  174.6 62.4 %all-gather.9.cloned.1.call-done = bf16[1024,5248]{1,0:T(8,128)(2,1)} async-done(((bf16[32,5248]{1,0:T(8,128)(2,1)}), bf16[1024,5248]{1,0:T(8,128)(2,1)}) %all-gather.9.cloned.1.call-update) | async-done | bytes 10747920 | tf_op jit(solution)/shard_map/all_gather | solution.py:167
  237.0 7.4 fusion.88
  244.4 60.1 %all-gather.11.cloned.1.call-done = bf16[1024,2624]{1,0:T(8,128)(2,1)} async-done(((bf16[32,2624]{1,0:T(8,128)(2,1)}), bf16[1024,2624]{1,0:T(8,128)(2,1)}) %all-gather.11.cloned.1.call-update) | async-done | bytes 5373968 | tf_op jit(solution)/shard_map/all_gather | solution.py:168
  304.5 6.8 fusion.46
  313.0 5.0 multiply_reduce_fusion.4
  322.9 3.6 all-to-all-start.2
  327.3 5.2 copy.127
  333.0 12.8 %reduce.23 = bf16[1024,1024]{1,0:T(8,128)(2,1)S(1)} reduce(bf16[1024,1,1024]{2,1,0:T(2,128)(2,1)} %bitcast.191, bf16[]{:T(256)} %broadcast.514), dimensions={1}, to_apply=%bitcast.178.reduce_sub_computation | reduce | bytes 4194306
  345.8 2.6 reshape.335
  348.3 4.8 all-to-all-start.6
  354.6 3.6 multiply_reduce_fusion
  366.3 5.0 fusion.1
  371.3 26.8 %copy.104 = bf16[1,1024,2624]{2,0,1:T(2,128)(2,1)} copy(bf16[1,1024,2624]{1,2,0:T(8,128)(2,1)} %fusion.1) | data formatting | bytes 10747904 | tf_op jit(solution)/shard_map/convert_element_type | solution.py:20
  398.2 34.3 %reduce.25 = bf16[1024,2624]{1,0:T(8,128)(2,1)} reduce(bf16[1024,1,2624]{2,1,0:T(2,128)(2,1)} %bitcast.186, bf16[]{:T(256)} %broadcast.514), dimensions={1}, to_apply=%bitcast.115.reduce_sub_computation | reduce | bytes 10747906
  432.5 9.3 reshape.327
  441.8 6.5 all-to-all-start.9
  448.4 3.2 fusion.32
  453.7 1.9 fusion.40
  455.6 1.7 fusion.41
  458.8 4.3 reshape.336
  463.1 3.0 copy.112
  466.1 1.7 reduce_sum.257
  471.9 3.6 copy.96
  475.6 33.8 %all-to-all-done.9 = bf16[2,2,671744]{2,1,0:T(2,128)(2,1)} async-done(((bf16[2,2,671744]{2,1,0:T(2,128)(2,1)}), bf16[2,2,671744]{2,1,0:T(2,128)(2,1)}, u32[]{:S(2)}, u32[]{:S(2)}) %all-to-all-start.9) | async-done | bytes 5373984 | tf_op jit(solution)/shard_map/all_to_all | solution.py:266
  509.3 4.7 all-to-all-start.3
  514.1 15.8 %reshape.328 = bf16[1024,1,2624]{2,1,0:T(2,128)(2,1)} reshape(bf16[2,2,671744]{2,1,0:T(2,128)(2,1)} %all-to-all-done.9) | data formatting | bytes 10747904
  529.9 7.3 copy.114
  537.3 5.9 reduce_sum.261
  546.4 1.8 convert_bitcast_fusion
  548.2 57.9 %copy.126 = bf16[1,1024,3072]{2,0,1:T(2,128)(2,1)} copy(bf16[1,1024,3072]{2,1,0:T(8,128)(2,1)S(1)} %convert_bitcast_fusion) | data formatting | bytes 12582912 | tf_op jit(solution)/shard_map/convert_element_type | solution.py:20
  606.1 37.8 %reduce.22 = bf16[1024,3072]{1,0:T(8,128)(2,1)} reduce(bf16[1024,1,3072]{2,1,0:T(2,128)(2,1)} %bitcast.185, bf16[]{:T(256)} %broadcast.514), dimensions={1}, to_apply=%bitcast.177.reduce_sub_computation | reduce | bytes 12582914
  643.9 8.1 reshape.333
  652.0 6.4 all-to-all-start.5
  658.4 5.1 fusion
  663.5 18.5 %copy.125 = bf16[1,1024,5248]{2,0,1:T(2,128)(2,1)} copy(bf16[1,1024,5248]{2,1,0:T(8,128)(2,1)S(1)} %fusion) | data formatting | bytes 21495808 | tf_op jit(solution)/shard_map/convert_element_type | solution.py:20
  682.0 66.9 %reduce.24 = bf16[1024,5248]{1,0:T(8,128)(2,1)} reduce(bf16[1024,1,5248]{2,1,0:T(2,128)(2,1)} %bitcast.180, bf16[]{:T(256)} %broadcast.514), dimensions={1}, to_apply=%bitcast.176.reduce_sub_computation | reduce | bytes 21495810
  748.9 12.7 %reshape.339 = bf16[2,2,1343488]{2,1,0:T(2,128)(2,1)} reshape(bf16[1024,5248]{1,0:T(8,128)(2,1)} %reduce.24) | data formatting | bytes 21495808
  761.6 7.7 all-to-all-start.8
  769.4 14.6 %reshape.334 = bf16[1024,1,3072]{2,1,0:T(2,128)(2,1)} reshape(bf16[2,2,786432]{2,1,0:T(2,128)(2,1)} %all-to-all-done.5) | data formatting | bytes 12582912
  783.9 9.6 copy.111
  793.5 6.7 reduce_sum.256
  800.3 87.5 %all-to-all-done.8 = bf16[2,2,1343488]{2,1,0:T(2,128)(2,1)} async-done(((bf16[2,2,1343488]{2,1,0:T(2,128)(2,1)}), bf16[2,2,1343488]{2,1,0:T(2,128)(2,1)}, u32[]{:S(2)}, u32[]{:S(2)}) %all-to-all-start.8) | async-done | bytes 10747936 | tf_op jit(solution)/shard_map/all_to_all | solution.py:266
  887.8 22.5 %reshape.340 = bf16[1024,1,5248]{2,1,0:T(2,128)(2,1)} reshape(bf16[2,2,1343488]{2,1,0:T(2,128)(2,1)} %all-to-all-done.8) | data formatting | bytes 21495808
  910.3 15.0 %copy.113 = bf16[1,1024,5248]{2,1,0:T(8,128)(2,1)} copy(bf16[1,1024,5248]{2,0,1:T(2,128)(2,1)} %bitcast.181) | data formatting | bytes 21495808
  925.4 9.6 reduce_sum.260
  938.1 3.4 all-to-all-start.7
  941.6 5.6 fusion.23
  948.8 5.5 multiply_reduce_fusion.6
  955.9 3.2 all-to-all-start.4
  960.3 2.6 all-to-all-done.4
  963.0 32.6 %all-reduce.7 = (bf16[512]{0:T(512)(128)(2,1)S(1)}, bf16[512]{0:T(512)(128)(2,1)S(1)}) all-reduce(bf16[512]{0:T(512)(128)(2,1)S(1)} %bitcast_reduce_fusion.1, bf16[512]{0:T(512)(128)(2,1)S(1)} %bitcast_reduce_fusion), channel_id=4, replica_groups=mesh['dp'=2,'ulysses'=8,'blk'=2] {'ulysses','blk'}, use_global_device_ids=true, to_apply=%region_18.19.clone | all-reduce | flops 1024 | bytes 4096
  998.5 1.7 convert_element_type.221
  1000.2 15.4 %reduce-scatter.17.cloned.1.call-done = bf16[32,5248]{1,0:T(8,128)(2,1)} async-done(((bf16[512,5248]{1,0:T(8,128)(2,1)}), bf16[32,5248]{1,0:T(8,128)(2,1)}) %reduce-scatter.17.cloned.1.call-update) | async-done | bytes 335888 | tf_op jit(solution)/shard_map/reduce_scatter | solution.py:278
  1015.6 1.9 convert_element_type.230
  (244 shorter events, 60.1 us)
Async XLA Ops:
  7.2 76.1 %all-gather.5.cloned.1.call-start = ((), (), s32[]{:S(2)}) async-start(), calls=%async_computation.16 | async-start | bytes 6488064 | tf_op jit(solution)/shard_map/all_gather | solution.py:164
  7.9 163.8 %all-gather.7.cloned.1.call-start = ((), (), s32[]{:S(2)}) async-start(), calls=%async_computation.17 | async-start | bytes 2162688 | tf_op jit(solution)/shard_map/all_gather | solution.py:165
  8.6 228.4 %all-gather.9.cloned.1.call-start = ((), (), s32[]{:S(2)}) async-start(), calls=%async_computation.18 | async-start | bytes 11083776 | tf_op jit(solution)/shard_map/all_gather | solution.py:167
  9.4 295.1 %all-gather.11.cloned.1.call-start = ((), (), s32[]{:S(2)}) async-start(), calls=%async_computation.19 | async-start | bytes 5677056 | tf_op jit(solution)/shard_map/all_gather | solution.py:168
  55.2 1.9 copy-start.39
  55.3 27.9 %copy-start.42 = (f32[128]{0:T(128)}, f32[128]{0:T(128)S(1)}, u32[]{:S(2)}) copy-start(f32[128]{0:T(128)S(1)} %div.81) | copy-start | bytes 1540
  57.7 25.6 %copy-start.44 = (f32[128]{0:T(128)}, f32[128]{0:T(128)S(1)}, u32[]{:S(2)}) copy-start(f32[128]{0:T(128)S(1)} %rsqrt.25) | copy-start | bytes 1540
  89.5 33.9 %all-to-all-start = ((bf16[2,64,16,192]{3,1,0,2:T(8,128)(2,1)}), bf16[2,64,16,192]{3,1,0,2:T(8,128)(2,1)S(1)}, u32[]{:S(2)}, u32[]{:S(2)}) async-start(bf16[2,64,16,192]{3,1,0,2:T(8,128)(2,1)} %copy.84), calls=%async_computation | async-start | bytes 2097152 | tf_op jit(solution)/shard_map/all_to_all | solution.py:177
  136.8 8.8 copy-start.16
  143.9 4.7 copy-start.22
  144.7 2.7 copy-start
  145.6 1.8 copy-start.35
  146.5 2.1 copy-start.2
  146.5 2.1 copy-start.29
  150.2 21.5 %copy-start.7 = (bf16[2,64,1024]{2,1,0:T(8,128)(2,1)S(1)}, bf16[2,64,1024]{2,1,0:T(8,128)(2,1)}, u32[]{:S(2)}) copy-start(bf16[2,64,1024]{2,1,0:T(8,128)(2,1)} %param.8) | copy-start | bytes 786436
  151.3 19.2 %all-to-all-start.1 = ((bf16[8,2,8192]{2,1,0:T(2,128)(2,1)}), bf16[8,2,8192]{2,1,0:T(2,128)(2,1)S(1)}, u32[]{:S(2)}, u32[]{:S(2)}) async-start(bf16[8,2,8192]{2,1,0:T(2,128)(2,1)} %reshape.325), calls=%async_computation.1 | async-start | bytes 524288 | tf_op jit(solution)/shard_map/all_to_all | solution.py:202
  171.6 3.0 copy-start.17
  173.9 144.1 %copy-start.31 = (f32[128]{0:T(128)}, f32[128]{0:T(128)S(1)}, u32[]{:S(2)}) copy-start(f32[128]{0:T(128)S(1)} %broadcast_multiply_fusion.1) | copy-start | bytes 1540
  237.0 76.0 %slice-start = ((s8[10747904]{0:T(1024)(128)(4,1)}), s8[2359296]{0:T(1024)(128)(4,1)S(1)}, s32[]{:S(2)}) async-start(s8[10747904]{0:T(1024)(128)(4,1)} %bitcast.182), calls=%async_computation.26 | async-start | bytes 4718592
  304.5 6.8 copy-start.10
  304.5 8.5 slice-start.1
  304.5 8.5 slice-start.2
  313.0 5.0 copy-start.8
  313.0 5.0 copy-start.50
  313.0 7.3 copy-start.19
  318.0 2.4 copy-start.12
  321.3 5.2 copy-start.36
  321.3 5.2 copy-start.30
  321.3 5.2 copy-start.38
  321.3 5.2 copy-start.18
  322.9 25.4 %all-to-all-start.2 = ((bf16[8,2,8192]{2,1,0:T(2,128)(2,1)}), bf16[8,2,8192]{2,1,0:T(2,128)(2,1)S(1)}, u32[]{:S(2)}, u32[]{:S(2)}) async-start(bf16[8,2,8192]{2,1,0:T(2,128)(2,1)} %reshape.329), calls=%async_computation.2 | async-start | bytes 524288 | tf_op jit(solution)/shard_map/all_to_all | solution.py:226
  348.3 93.5 %all-to-all-start.6 = ((bf16[2,2,262144]{2,1,0:T(2,128)(2,1)}), bf16[2,2,262144]{2,1,0:T(2,128)(2,1)}, u32[]{:S(2)}, u32[]{:S(2)}) async-start(bf16[2,2,262144]{2,1,0:T(2,128)(2,1)} %reshape.335), calls=%async_computation.9 | async-start | bytes 4194304 | tf_op jit(solution)/shard_map/all_to_all | solution.py:266
  353.2 114.7 %reduce-scatter.9.cloned.1.call-start = ((), (), s32[]{:S(2)}) async-start(), calls=%async_computation.20 | async-start | bytes 786432 | tf_op jit(solution)/shard_map/reduce_scatter | solution.py:243
  354.3 3.9 copy-start.27
  354.6 4.8 copy-start.25
  354.6 3.7 copy-start.1
  358.2 2.2 copy-start.3
  358.3 2.3 copy-start.24
  441.8 6.6 copy-start.28
  441.8 67.5 %all-to-all-start.9 = ((bf16[2,2,671744]{2,1,0:T(2,128)(2,1)}), bf16[2,2,671744]{2,1,0:T(2,128)(2,1)}, u32[]{:S(2)}, u32[]{:S(2)}) async-start(bf16[2,2,671744]{2,1,0:T(2,128)(2,1)} %reshape.327), calls=%async_computation.14 | async-start | bytes 10747904 | tf_op jit(solution)/shard_map/all_to_all | solution.py:266
  448.4 3.3 copy-start.26
  448.4 21.9 %reduce-scatter.11.cloned.1.call-start = ((), (), s32[]{:S(2)}) async-start(), calls=%async_computation.21 | async-start | bytes 786432 | tf_op jit(solution)/shard_map/reduce_scatter | solution.py:246
  448.4 3.5 copy-start.4
  453.7 493.5 %reduce-scatter.15.cloned.1.call-start = ((), (), s32[]{:S(2)}) async-start(), calls=%async_computation.23 | async-start | bytes 1114112 | tf_op jit(solution)/shard_map/reduce_scatter | solution.py:278
  453.7 1.9 copy-start.6
  509.3 34.8 %all-to-all-start.3 = ((bf16[2,512,2,192]{3,2,0,1:T(2,128)(2,1)}), bf16[2,512,2,192]{3,2,0,1:T(2,128)(2,1)S(1)}, u32[]{:S(2)}, u32[]{:S(2)}) async-start(bf16[2,512,2,192]{3,2,0,1:T(2,128)(2,1)} %copy.96), calls=%async_computation.5 | async-start | bytes 2097152 | tf_op jit(solution)/shard_map/all_to_all | solution.py:258
  514.1 482.1 %reduce-scatter.19.cloned.1.call-start = ((), (), s32[]{:S(2)}) async-start(), calls=%async_computation.25 | async-start | bytes 2924544
  652.0 6.4 copy-start.9
  652.0 6.5 copy-start.32
  652.0 6.5 copy-start.34
  652.0 109.6 %all-to-all-start.5 = ((bf16[2,2,786432]{2,1,0:T(2,128)(2,1)}), bf16[2,2,786432]{2,1,0:T(2,128)(2,1)}, u32[]{:S(2)}, u32[]{:S(2)}) async-start(bf16[2,2,786432]{2,1,0:T(2,128)(2,1)} %reshape.333), calls=%async_computation.7 | async-start | bytes 12582912 | tf_op jit(solution)/shard_map/all_to_all | solution.py:266
  761.6 126.3 %all-to-all-start.8 = ((bf16[2,2,1343488]{2,1,0:T(2,128)(2,1)}), bf16[2,2,1343488]{2,1,0:T(2,128)(2,1)}, u32[]{:S(2)}, u32[]{:S(2)}) async-start(bf16[2,2,1343488]{2,1,0:T(2,128)(2,1)} %reshape.339), calls=%async_computation.12 | async-start | bytes 21495808 | tf_op jit(solution)/shard_map/all_to_all | solution.py:266
  769.3 229.1 %reduce-scatter.13.cloned.1.call-start = ((), (), s32[]{:S(2)}) async-start(), calls=%async_computation.22 | async-start | bytes 3342336 | tf_op jit(solution)/shard_map/reduce_scatter | solution.py:278
  800.3 215.4 %reduce-scatter.17.cloned.1.call-start = ((), (), s32[]{:S(2)}) async-start(), calls=%async_computation.24 | async-start | bytes 5709824 | tf_op jit(solution)/shard_map/reduce_scatter | solution.py:278
  935.0 1.9 copy-start.41
  935.0 6.6 copy-start.11
  938.1 9.0 all-to-all-start.7
  941.5 7.2 copy-start.43
  948.7 5.6 copy-start.53
  948.7 5.6 copy-start.45
  948.7 10.4 %copy-start.15 = (f32[128,1024]{1,0:T(8,128)S(1)}, f32[128,1024]{1,0:T(8,128)}, u32[]{:S(2)}) copy-start(f32[128,1024]{1,0:T(8,128)} %copy-done.14) | copy-start | bytes 1572868
  948.7 10.5 %copy-start.21 = (bf16[2,64,1024]{2,1,0:T(8,128)(2,1)S(1)}, bf16[2,64,1024]{2,1,0:T(8,128)(2,1)}, u32[]{:S(2)}) copy-start(bf16[2,64,1024]{2,1,0:T(8,128)(2,1)} %param.15) | copy-start | bytes 786436
  948.8 10.4 %copy-start.48 = (f32[128]{0:T(128)S(1)}, f32[128]{0:T(128)}, u32[]{:S(2)}) copy-start(f32[128]{0:T(128)} %copy-done.47) | copy-start | bytes 1540
  955.9 7.0 all-to-all-start.4
  (13 other events, 13.5 us)
Sparse Core Ops, SparseCore 0:
  10.9 72.2 all-gather.4
  86.2 58.0 all-gather.6
  147.1 89.9 all-gather.8
  239.8 64.6 all-gather.10
  366.4 16.3 reduce-scatter.8
  453.8 16.4 reduce-scatter.10
  473.9 58.0 reduce-scatter.14
  543.3 64.8 reduce-scatter.18
  800.4 67.8 reduce-scatter.12
  935.1 80.4 reduce-scatter.16
where the time goes:
time: 1040 us; the launch traced here: 1020 us
  waiting for transfers between devices  334 us (32%)
  local copies, waits for them, and re-layouts  261 us (25%)
  other arithmetic  203 us (20%)
  blocking collectives  94.3 us (9%)
  matrix products  67.4 us (6%)
  starting transfers between devices  48.4 us (5%)
  between operations  16.1 us (2%)
    unnamed x11, other arithmetic  156 us
    unnamed x145, local copies, waits for them, and re-layouts  140 us
    all_to_all x6, waiting for transfers between devices, body(): lax.all_to_all(as_sent(stack_front((grad_gain_attn, grad_qkv, grad_out, g...  124 us
    convert_element_type x6, local copies, waits for them, and re-layouts, short(): return part.astype(jnp.bfloat16) if part.dtype == jnp.float32 else part  108 us
    unnamed x2, blocking collectives  75.1 us
    all_gather x1, waiting for transfers between devices, body(): lax.all_gather(input_projection_weight, ('dp', 'ulysses', 'blk'), axis=0,...  62.4 us
    all_gather x1, waiting for transfers between devices, body(): lax.all_gather(down_projection_weight, ('dp', 'ulysses', 'blk'), axis=0,...  60.1 us
    all_to_all x6, starting transfers between devices, body(): lax.all_to_all(as_sent(stack_front((grad_gain_attn, grad_qkv, grad_out, g...  32.1 us
  transfers between devices with their start and end apart: 20, of which 9 were waited for; matrix products, arithmetic and copies ran while one was open for 49% of the time, Pallas kernels for 0%

commit v1 on v0

v1 whole, which is shorter than its diff:
```python
import math

import jax
import jax.numpy as jnp
from jax import lax
from jax.experimental import pallas as pl
from jax.experimental.pallas import tpu as pltpu
from jax.sharding import PartitionSpec as P

FF = 2624
HEADS = 16
HEAD_DIM = 64


EPSILON = 1e-05
ROPE_BASE = 160000.0


def layer_norm(values, gain):
    average = jnp.mean(values, axis=-1, keepdims=True)
    centered = values - average
    variance = jnp.mean(centered * centered, axis=-1, keepdims=True)
    return centered * lax.rsqrt(variance + EPSILON) * gain


def rope_tables(positions, half_dim):
    ladder = jnp.arange(half_dim, dtype=jnp.float32)
    frequency = ROPE_BASE ** (-2.0 * ladder / (2 * half_dim))
    angles = positions[:, None] * frequency[None, :]
    return (jnp.cos(angles)[:, None, :], jnp.sin(angles)[:, None, :])


def rotate(values, cosine, sine):
    half_dim = values.shape[-1] // 2
    first_half = values[..., :half_dim]
    second_half = values[..., half_dim:]
    return jnp.concatenate(
        [first_half * cosine - second_half * sine, second_half * cosine + first_half * sine],
        axis=-1,
    )


def rotate_back(gradient, cosine, sine):
    half_dim = gradient.shape[-1] // 2
    first_half = gradient[..., :half_dim]
    second_half = gradient[..., half_dim:]
    return jnp.concatenate(
        [first_half * cosine + second_half * sine, second_half * cosine - first_half * sine],
        axis=-1,
    )


def contract_rows(left_side, right_side):
    return lax.dot_general(
        left_side, right_side, (((0,), (0,)), ((), ())), preferred_element_type=jnp.float32
    )


def contract_cols(left_side, right_side):
    return lax.dot_general(
        left_side, right_side, (((1,), (1,)), ((), ())), preferred_element_type=jnp.float32
    )


BF = jnp.bfloat16
MESH = pl.DeviceIdType.MESH


def exchange(x, axes, cid):
    sizes = [lax.axis_size(a) for a in axes]
    n = math.prod(sizes)

    def kernel(x_ref, o_ref, send, recv, local):
        me = 0
        for a, s in zip(axes, sizes):
            me = me * s + lax.axis_index(a)

        def place(k):
            ids = {}
            for a, s in reversed(list(zip(axes, sizes))):
                ids[a] = lax.rem(k, s)
                k = k // s
            return ids

        barrier = pltpu.get_barrier_semaphore()
        for k in range(1, n):
            pl.semaphore_signal(
                barrier, 1, device_id=place(lax.rem(me + k, n)), device_id_type=MESH
            )
        pl.semaphore_wait(barrier, n - 1)
        copies = []
        for k in range(1, n):
            peer = lax.rem(me + k, n)
            copy = pltpu.make_async_remote_copy(
                src_ref=x_ref.at[peer],
                dst_ref=o_ref.at[me],
                send_sem=send.at[k],
                recv_sem=recv.at[k],
                device_id=place(peer),
                device_id_type=MESH,
            )
            copy.start()
            copies.append(copy)
        own = pltpu.make_async_copy(x_ref.at[me], o_ref.at[me], local)
        own.start()
        own.wait()
        for copy in copies:
            copy.wait()

    return pl.pallas_call(
        kernel,
        out_shape=jax.ShapeDtypeStruct(x.shape, x.dtype),
        in_specs=[pl.BlockSpec(memory_space=pl.ANY)],
        out_specs=pl.BlockSpec(memory_space=pl.ANY),
        scratch_shapes=[
            pltpu.SemaphoreType.DMA((n,)),
            pltpu.SemaphoreType.DMA((n,)),
            pltpu.SemaphoreType.DMA,
        ],
        compiler_params=pltpu.CompilerParams(collective_id=cid, has_side_effects=True),
    )(x)


def gather_line(x, cid):
    n = lax.axis_size("ulysses")
    chips = n // 2

    def kernel(x_ref, o_ref, send, recv, pass_send, pass_recv, local):
        me = lax.axis_index("ulysses")
        chip, core = me // 2, lax.rem(me, 2)
        partner = chip * 2 + (1 - core)
        barrier = pltpu.get_barrier_semaphore()
        pl.semaphore_signal(barrier, 1, device_id={"ulysses": partner}, device_id_type=MESH)
        for k in range(1, chips):
            peer = lax.rem(chip + k, chips) * 2 + core
            pl.semaphore_signal(barrier, 1, device_id={"ulysses": peer}, device_id_type=MESH)
        pl.semaphore_wait(barrier, chips)
        far = []
        for k in range(1, chips):
            peer = lax.rem(chip + k, chips) * 2 + core
            copy = pltpu.make_async_remote_copy(
                src_ref=x_ref,
                dst_ref=o_ref.at[me],
                send_sem=send.at[k],
                recv_sem=recv.at[k],
                device_id={"ulysses": peer},
                device_id_type=MESH,
            )
            copy.start()
            far.append(copy)
        near = [
            pltpu.make_async_remote_copy(
                src_ref=x_ref,
                dst_ref=o_ref.at[me],
                send_sem=pass_send.at[0],
                recv_sem=pass_recv.at[0],
                device_id={"ulysses": partner},
                device_id_type=MESH,
            )
        ]
        near[0].start()
        own = pltpu.make_async_copy(x_ref, o_ref.at[me], local)
        own.start()
        for k in range(1, chips):
            far[k - 1].wait_recv()
            slot = lax.rem(chip - k + chips, chips) * 2 + core
            copy = pltpu.make_async_remote_copy(
                src_ref=o_ref.at[slot],
                dst_ref=o_ref.at[slot],
                send_sem=pass_send.at[k],
                recv_sem=pass_recv.at[k],
                device_id={"ulysses": partner},
                device_id_type=MESH,
            )
            copy.start()
            near.append(copy)
        own.wait()
        for copy in far:
            copy.wait_send()
        for copy in near:
            copy.wait()

    return pl.pallas_call(
        kernel,
        out_shape=jax.ShapeDtypeStruct((n,) + x.shape, x.dtype),
        in_specs=[pl.BlockSpec(memory_space=pl.ANY)],
        out_specs=pl.BlockSpec(memory_space=pl.ANY),
        scratch_shapes=[pltpu.SemaphoreType.DMA((chips,))] * 4 + [pltpu.SemaphoreType.DMA],
        compiler_params=pltpu.CompilerParams(collective_id=cid, has_side_effects=True),
    )(x)


def scatter_line(x, cid):
    n, rows, cols = x.shape
    chips = n // 2

    def kernel(x_ref, o_ref, pair, summed, land, send, recv, pass_send, pass_recv):
        me = lax.axis_index("ulysses")
        chip, core = me // 2, lax.rem(me, 2)
        partner = chip * 2 + (1 - core)
        barrier = pltpu.get_barrier_semaphore()
        pl.semaphore_signal(barrier, 1, device_id={"ulysses": partner}, device_id_type=MESH)
        for k in range(1, chips):
            peer = lax.rem(chip + k, chips) * 2 + core
            pl.semaphore_signal(barrier, 1, device_id={"ulysses": peer}, device_id_type=MESH)
        pl.semaphore_wait(barrier, chips)
        order = list(range(1, chips)) + [0]
        near, far = {}, {}
        for k in order:
            there = lax.rem(chip + k, chips)
            near[k] = pltpu.make_async_remote_copy(
                src_ref=x_ref.at[there * 2 + (1 - core)],
                dst_ref=pair.at[k],
                send_sem=pass_send.at[k],
                recv_sem=pass_recv.at[k],
                device_id={"ulysses": partner},
                device_id_type=MESH,
            )
            near[k].start()
        for k in order:
            there = lax.rem(chip + k, chips)
            near[k].wait_recv()
            total = x_ref[there * 2 + core].astype(jnp.float32) + pair[k].astype(jnp.float32)
            if k == 0:
                o_ref[...] = total
            else:
                summed[k] = total.astype(BF)
                far[k] = pltpu.make_async_remote_copy(
                    src_ref=summed.at[k],
                    dst_ref=land.at[k],
                    send_sem=send.at[k],
                    recv_sem=recv.at[k],
                    device_id={"ulysses": there * 2 + core},
                    device_id_type=MESH,
                )
                far[k].start()
        for k in range(1, chips):
            far[k].wait_recv()
            o_ref[...] += land[k].astype(jnp.float32)
        for k in order:
            near[k].wait_send()
            if k:
                far[k].wait_send()

    block = pltpu.VMEM((chips, rows, cols), BF)
    return pl.pallas_call(
        kernel,
        out_shape=jax.ShapeDtypeStruct((rows, cols), jnp.float32),
        in_specs=[pl.BlockSpec(memory_space=pltpu.VMEM)],
        out_specs=pl.BlockSpec(memory_space=pltpu.VMEM),
        scratch_shapes=[block] * 3 + [pltpu.SemaphoreType.DMA((chips,))] * 4,
        compiler_params=pltpu.CompilerParams(
            collective_id=cid, has_side_effects=True, vmem_limit_bytes=40 * 1024 * 1024
        ),
    )(x)


def pad_to(x, cols):
    return jnp.pad(x, [(0, 0)] * (x.ndim - 1) + [(0, cols - x.shape[-1])])


def body(
    tokens,
    norm_gain_attn,
    query_key_value_weight,
    attention_output_weight,
    norm_gain_mlp,
    input_projection_weight,
    down_projection_weight,
    cotangent,
):
    seq_count, local_len, width = tokens.shape
    n_dp, n_u, n_b = (lax.axis_size(a) for a in ("dp", "ulysses", "blk"))
    part = width // (n_dp * n_u * n_b)
    heads = HEADS // n_u
    head_cols = heads * 3 * HEAD_DIM
    ff_cols = FF // n_u
    ff_pad = -(-ff_cols // 128) * 128
    rows = seq_count * local_len
    length = rows * n_u
    f32 = jnp.float32

    qkv_cut = query_key_value_weight.reshape(part, n_u, head_cols).transpose(1, 0, 2)
    gains = jnp.stack([norm_gain_attn, norm_gain_mlp], axis=1)
    gains = jnp.broadcast_to(pad_to(gains, 128)[None], (n_u, part, 128))
    first_cut = jnp.concatenate([qkv_cut, gains], axis=2)
    in_cut = pad_to(input_projection_weight.reshape(part, 2, n_u, ff_cols), ff_pad)
    in_cut = in_cut.transpose(2, 0, 1, 3).reshape(n_u, part, 2 * ff_pad)
    down_cut = pad_to(down_projection_weight.reshape(part, n_u, ff_cols), ff_pad)
    mlp_cut = jnp.concatenate([in_cut, down_cut.transpose(1, 0, 2)], axis=2)

    def in_order(gathered):
        cols = gathered.shape[-1]
        gathered = gathered.reshape(n_dp, n_b, n_u, part, cols)
        return gathered.transpose(0, 2, 1, 3, 4).reshape(width, cols)

    def by_owner(grads):
        cols = grads.shape[-1]
        grads = grads.reshape(n_dp, n_u, n_b, part, cols).transpose(0, 2, 1, 3, 4)
        return grads.reshape(n_dp * n_b, n_u * part, cols)

    first_cut = exchange(first_cut, ("ulysses",), 1)
    mlp_cut = lax.all_to_all(mlp_cut, "ulysses", 0, 0)
    mlp_full = in_order(
        lax.all_gather(mlp_cut.reshape(n_u * part, -1), ("dp", "blk"), axis=0, tiled=True)
    )
    out_full = lax.all_gather(
        attention_output_weight, ("dp", "ulysses", "blk"), axis=0, tiled=True
    )
    copies = jnp.broadcast_to(
        first_cut.reshape(1, n_u * part, -1), (n_dp * n_b, n_u * part, head_cols + 128)
    )
    first_full = in_order(exchange(copies, ("dp", "blk"), 2))
    qkv_w = first_full[:, :head_cols]
    gain_attn_f = first_full[:, head_cols].astype(f32)
    gain_mlp_f = first_full[:, head_cols + 1].astype(f32)
    in_w = mlp_full[:, : 2 * ff_pad]
    down_w = mlp_full[:, 2 * ff_pad :]

    both = exchange(jnp.stack([tokens, cotangent], axis=1), ("blk",), 3)
    inputs_low = both[:, 0].reshape(rows, width)
    grad_top = both[:, 1].reshape(rows, width)
    inputs = inputs_low.astype(f32)
    tokens_all = gather_line(inputs_low, 4).reshape(length, width)
    cot_all = lax.all_gather(grad_top, "ulysses", axis=0, tiled=True)
    normed = layer_norm(tokens_all.astype(f32), gain_attn_f).astype(BF)
    joined = jnp.dot(normed, qkv_w, preferred_element_type=f32).astype(BF)
    joined = joined.reshape(length, heads, 3 * HEAD_DIM)
    cosine, sine = rope_tables(jnp.arange(length, dtype=f32), HEAD_DIM // 2)
    queries = rotate(joined[..., :HEAD_DIM].astype(f32), cosine, sine).astype(BF)
    keys = rotate(joined[..., HEAD_DIM : 2 * HEAD_DIM].astype(f32), cosine, sine).astype(BF)
    queries, keys = queries.transpose(1, 0, 2), keys.transpose(1, 0, 2)
    values = joined[..., 2 * HEAD_DIM :].transpose(1, 0, 2)
    scale = 1.0 / math.sqrt(HEAD_DIM)

    def probs_of(queries, keys):
        scores = jnp.einsum("hqe,hke->hqk", queries, keys, preferred_element_type=f32) * scale
        exponent = jnp.exp(scores - jnp.max(scores, axis=-1, keepdims=True))
        return exponent / jnp.sum(exponent, axis=-1, keepdims=True)

    weights = probs_of(queries, keys)
    probs = weights.astype(BF)
    attended = jnp.einsum("hqk,hke->qhe", probs, values, preferred_element_type=f32)
    attended = attended.astype(BF).reshape(n_u, rows, heads * HEAD_DIM)
    back = exchange(attended, ("ulysses",), 5).transpose(1, 0, 2).reshape(rows, width)

    middle = inputs + jnp.dot(back, out_full, preferred_element_type=f32)
    normed_mlp_own = layer_norm(middle, gain_mlp_f).astype(BF)
    normed_mlp = gather_line(normed_mlp_own, 6).reshape(length, width)
    hidden = jnp.dot(normed_mlp, in_w, preferred_element_type=f32)

    def gated(hidden):
        return jax.nn.gelu(hidden[:, :ff_pad], approximate=False) * hidden[:, ff_pad:]

    active, gated_pull = jax.vjp(gated, hidden)
    active = active.astype(BF)
    grad_active = jnp.dot(cot_all, down_w, preferred_element_type=f32)
    grad_hidden = gated_pull(grad_active)[0].astype(BF)
    grad_normed = contract_cols(grad_hidden, in_w).astype(BF)
    grad_normed = scatter_line(grad_normed.reshape(n_u, rows, width), 7)
    mlp_part = contract_cols(active, down_w).astype(BF)
    mlp_sum = lax.psum_scatter(mlp_part, "ulysses", scatter_dimension=0, tiled=True)
    grad_in = contract_rows(normed_mlp, grad_hidden)
    grad_down = contract_rows(cot_all, active)
    mlp_grads = jnp.concatenate([grad_in, grad_down], axis=1).astype(BF)
    mlp_grads = lax.psum_scatter(
        by_owner(mlp_grads).reshape(width, -1), ("dp", "blk"), scatter_dimension=0, tiled=True
    )

    _, norm_pull = jax.vjp(layer_norm, middle, gain_mlp_f)
    grad_middle, gain_mlp_part = norm_pull(grad_normed)
    grad_middle = grad_top.astype(f32) + grad_middle
    grad_branch = grad_middle.astype(BF)
    grad_back = contract_cols(grad_branch, out_full).astype(BF)
    grad_back = grad_back.reshape(rows, n_u, heads * HEAD_DIM).transpose(1, 0, 2)
    grad_heads = exchange(grad_back, ("ulysses",), 8).reshape(length, heads, HEAD_DIM)
    grad_heads = grad_heads.transpose(1, 0, 2)
    grad_out = lax.psum_scatter(
        contract_rows(back, grad_branch).astype(BF),
        ("dp", "ulysses", "blk"),
        scatter_dimension=0,
        tiled=True,
    ).astype(f32)

    grad_values = jnp.einsum("hqk,hqe->khe", probs, grad_heads, preferred_element_type=f32)
    grad_probs = jnp.einsum("hqe,hke->hqk", grad_heads, values, preferred_element_type=f32)
    inner = jnp.sum(weights * grad_probs, axis=-1, keepdims=True)
    grad_scores = (weights * (grad_probs - inner)).astype(BF)
    grad_q = jnp.einsum("hqk,hke->qhe", grad_scores, keys, preferred_element_type=f32) * scale
    grad_k = jnp.einsum("hqk,hqe->khe", grad_scores, queries, preferred_element_type=f32) * scale
    grad_joined = jnp.concatenate(
        [rotate_back(grad_q, cosine, sine), rotate_back(grad_k, cosine, sine), grad_values],
        axis=-1,
    )
    grad_joined = grad_joined.astype(BF).reshape(length, head_cols)
    grad_first = contract_cols(grad_joined, qkv_w).astype(BF)
    grad_first = scatter_line(grad_first.reshape(n_u, rows, width), 9)
    _, first_pull = jax.vjp(layer_norm, inputs, gain_attn_f)
    grad_input, gain_attn_part = first_pull(grad_first)
    input_grad = grad_middle + grad_input
    output = middle + mlp_sum.astype(f32)
    ends = jnp.stack([output.astype(BF), input_grad.astype(BF)], axis=0)
    ends = ends.reshape(2, seq_count, local_len, width).transpose(1, 0, 2, 3)
    ends = exchange(ends, ("blk",), 10)
    output, input_grad = ends[:, 0], ends[:, 1].astype(f32)

    gain_parts = pad_to(jnp.stack([gain_attn_part, gain_mlp_part], axis=1), 128)
    first_grads = jnp.concatenate([contract_rows(normed, grad_joined), gain_parts], axis=1)
    first_grads = exchange(by_owner(first_grads.astype(BF)), ("dp", "blk"), 11)
    first_grads = jnp.sum(first_grads.astype(f32), axis=0).astype(BF)
    last = jnp.concatenate([first_grads, mlp_grads], axis=1).reshape(n_u, part, -1)
    last = exchange(last, ("ulysses",), 12)
    gain_sums = jnp.sum(last[:, :, head_cols : head_cols + 2].astype(f32), axis=0)
    grad_qkv = last[:, :, :head_cols].transpose(1, 0, 2).reshape(part, -1).astype(f32)
    at = head_cols + 128
    grad_in = last[:, :, at : at + 2 * ff_pad].reshape(n_u, part, 2, ff_pad)[..., :ff_cols]
    grad_in = grad_in.transpose(1, 2, 0, 3).reshape(part, -1).astype(f32)
    grad_down = last[:, :, at + 2 * ff_pad :][..., :ff_cols]
    grad_down = grad_down.transpose(1, 0, 2).reshape(part, -1).astype(f32)
    return (
        output,
        input_grad,
        gain_sums[:, 0],
        grad_qkv,
        grad_out,
        gain_sums[:, 1],
        grad_in,
        grad_down,
    )


def solution(mesh):
    in_specs = (
        P("dp", ("ulysses", "blk"), None),
        P(("dp", "ulysses", "blk")),
        P(("dp", "ulysses", "blk"), None),
        P(("dp", "ulysses", "blk"), None),
        P(("dp", "ulysses", "blk")),
        P(("dp", "ulysses", "blk"), None),
        P(("dp", "ulysses", "blk"), None),
        P("dp", ("ulysses", "blk"), None),
    )
    out_specs = (
        P("dp", ("ulysses", "blk"), None),
        P("dp", ("ulysses", "blk"), None),
        P(("dp", "ulysses", "blk")),
        P(("dp", "ulysses", "blk"), None),
        P(("dp", "ulysses", "blk"), None),
        P(("dp", "ulysses", "blk")),
        P(("dp", "ulysses", "blk"), None),
        P(("dp", "ulysses", "blk"), None),
    )
    return jax.shard_map(body, mesh=mesh, in_specs=in_specs, out_specs=out_specs, check_vma=False)
```

time: 1040 us -> 439 us (0.42)
  waiting for transfers between devices: 334 us -> 44.8 us
  Pallas kernels: 0 us -> 230 us
  local copies, waits for them, and re-layouts: 261 us -> 39.2 us
  other arithmetic: 203 us -> 33.7 us
  blocking collectives: 94.3 us -> 24.5 us
  starting transfers between devices: 48.4 us -> 0.24 us
  matrix products: 67.4 us -> 44.8 us
    pallas_call x0 -> x12, Pallas kernels: none -> 230 us  [the longest x8 122 us: exchange(): pl.pallas_call(kernel, out_shape=jax.ShapeDtypeStruct(x.shape, x.dtype),...]
    all_to_all x10 -> x0, waiting for transfers between devices: 169 us -> none  [the longest x6 124 us: body(): lax.all_to_all(as_sent(stack_front((grad_gain_attn, grad_qkv, grad_out, g...]
    unnamed x11 -> x5, other arithmetic: 156 us -> 0.25 us
    all_gather x3 -> x2, waiting for transfers between devices: 147 us -> 0.02 us  [the longest x1 0.02 us: body(): lax.all_gather(mlp_cut.reshape(n_u * part, -1), ('dp', 'blk'), axis=0, ti...]
    unnamed x145 -> x105, local copies, waits for them, and re-layouts: 140 us -> 7.7 us
    convert_element_type x6, local copies, waits for them, and re-layouts: 108 us -> 3.7 us  [the longest x2 1.63 us: body(): grad_in = grad_in.transpose(1, 2, 0, 3).reshape(part, -1).astype(f32)]
    unnamed x2 -> x0, blocking collectives: 75.1 us -> none
    all_to_all x10 -> x0, starting transfers between devices: 47.8 us -> none  [the longest x6 32.1 us: body(): lax.all_to_all(as_sent(stack_front((grad_gain_attn, grad_qkv, grad_out, g...]
  transfers between devices with their start and end apart: 20 -> 6, of which waited for: 9 -> 1; matrix products, arithmetic and copies ran while one was open for 49% -> 25% of each run, Pallas kernels for 0% -> 53%
where the time goes in v1:
time: 439 us; the launch traced here: 433 us
  Pallas kernels  230 us (52%)
  waiting for transfers between devices  44.8 us (10%)
  matrix products  44.8 us (10%)
  local copies, waits for them, and re-layouts  39.2 us (9%)
  other arithmetic  33.7 us (8%)
  blocking collectives  24.5 us (6%)
  between operations  15.6 us (4%)
    pallas_call x8, Pallas kernels, exchange(): pl.pallas_call(kernel, out_shape=jax.ShapeDtypeStruct(x.shape, x.dtype),...  122 us
    pallas_call x2, Pallas kernels, scatter_line(): pl.pallas_call(kernel, out_shape=jax.ShapeDtypeStruct((rows, cols), jnp.f...  56 us
    pallas_call x2, Pallas kernels, gather_line(): pl.pallas_call(kernel, out_shape=jax.ShapeDtypeStruct((n,) + x.shape, x.d...  51.6 us
    reduce_scatter x1, waiting for transfers between devices, body(): lax.psum_scatter(contract_rows(back, grad_branch).astype(BF), ('dp', 'uly...  43.9 us
    all_to_all x1, blocking collectives, body(): mlp_cut = lax.all_to_all(mlp_cut, 'ulysses', 0, 0)  24.5 us
  transfers between devices with their start and end apart: 6, of which 1 were waited for; matrix products, arithmetic and copies ran while one was open for 25% of the time, Pallas kernels for 53%

profile of v1, /device:TPU:0, one launch (start us, length us, event | category | flops | bytes accessed | tf_op | source)
XLA Modules:
  0.0 432.6 jit_solution(13642833072307175843)
XLA Ops:
  7.9 1.2 reshape.312
  9.2 1.7 reshape.310
  11.9 24.5 %all_to_all.5 = bf16[8,32,1152]{2,1,0:T(8,128)(2,1)} all-to-all(bf16[8,32,1152]{2,1,0:T(8,128)(2,1)S(1)} %pad_maximum_fusion.1), channel_id=1, replica_groups=mesh['dp'=2,'ulysses'=8,'blk'=2] {'ulysses'}, dimensions={0} | all-to-all | bytes 1179648 | tf_op jit(solution)/shard_map/all_to_all | solution.py:303
  37.4 10.6 %shard_map.143 = bf16[2,2,64,1024]{3,2,1,0:T(8,128)(2,1)} custom-call(bf16[2,2,64,1024]{3,2,1,0:T(8,128)(2,1)} %pad_maximum_fusion.2.x_ref), custom_call_target="tpu_custom_call" | custom-call | tf_op jit(solution)/shard_map/pallas_call | solution.py:110
  48.0 1.9 fusion.72
  50.9 8.2 %shard_map.145 = bf16[8,32,512]{2,1,0:T(8,128)(2,1)} custom-call(bf16[8,32,512]{2,1,0:T(8,128)(2,1)} %pad_maximum_fusion.3.x_ref), custom_call_target="tpu_custom_call" | custom-call | tf_op jit(solution)/shard_map/pallas_call | solution.py:110
  59.6 2.1 broadcast_in_dim.16.x_ref
  61.6 16.0 %shard_map.146 = bf16[4,256,512]{2,1,0:T(8,128)(2,1)} custom-call(bf16[4,256,512]{2,1,0:T(8,128)(2,1)} %broadcast_in_dim.16.x_ref), custom_call_target="tpu_custom_call" | custom-call | tf_op jit(solution)/shard_map/pallas_call | solution.py:110
  77.6 1.3 copy.101
  79.0 1.0 copy-done.15
  80.2 23.7 %shard_map.144 = bf16[8,128,1024]{2,1,0:T(8,128)(2,1)} custom-call(bf16[128,1024]{1,0:T(8,128)(2,1)} %bitcast.173), custom_call_target="tpu_custom_call" | custom-call | tf_op jit(solution)/shard_map/pallas_call | solution.py:183
  104.0 2.1 convert_reduce_fusion
  108.1 1.0 convolution_convert_fusion.7
  110.1 5.1 %fusion.73 = (f32[2,1024]{1,0:T(2,128)S(1)}, f32[2,1024,1024]{1,2,0:T(8,128)}) fusion(bf16[1024,2,32]{0,2,1:T(8,128)(2,1)S(1)} %get-tuple-element.33, bf16[1024,2,32]{0,2,1:T(8,128)(2,1)S(1)} %get-tuple-element.34, bf16[1024,2,32]{0,2,1:T(8,128)(2,1)S(1)} %get-tuple-element.23, bf16[1024,2,32]{0,2,1:T(8,128)(2,1)S(1)} %get-tuple-element.22), kind=kOutput, calls=%fused_computation.154 | convolution fusion | flops 275776512 | bytes 8921088 | tf_op jit(solution)/shard_map/sub | solution.py:338
  115.2 4.3 %fusion.31 = bf16[2,64,1024]{2,1,0:T(8,128)(2,1)S(1)} fusion(bf16[1024,2,192]{0,2,1:T(8,128)(2,1)} %bitcast.207, f32[2,1024,1024]{1,2,0:T(8,128)} %get-tuple-element.44, f32[2,1024]{1,0:T(2,128)S(1)} %get-tuple-element.43), kind=kOutput, calls=%fused_computation.59 | convolution fusion | flops 272760832 | bytes 8921088 | tf_op jit(solution)/shard_map/hqk,hke->qhe/dot_general | solution.py:343
  119.6 0.9 copy.103.x_ref
  120.5 16.4 %shard_map.147 = bf16[8,128,128]{2,1,0:T(8,128)(2,1)} custom-call(bf16[8,128,128]{2,1,0:T(8,128)(2,1)} %copy.103.x_ref), custom_call_target="tpu_custom_call" | custom-call | tf_op jit(solution)/shard_map/pallas_call | solution.py:110
  137.0 1.1 copy.104
  138.2 2.2 fusion.74
  140.6 0.8 multiply_convert_fusion.3.x_ref
  141.5 27.9 %shard_map.148 = bf16[8,128,1024]{2,1,0:T(8,128)(2,1)} custom-call(bf16[128,1024]{1,0:T(8,128)(2,1)} %multiply_convert_fusion.3.x_ref), custom_call_target="tpu_custom_call" | custom-call | tf_op jit(solution)/shard_map/pallas_call | solution.py:183
  169.4 2.1 copy.107
  171.7 1.8 fusion.21
  173.5 4.4 %multiply_convert_fusion.2 = (bf16[1024,384]{1,0:T(8,128)(2,1)S(1)}, f32[1024,384]{1,0:T(8,128)}) fusion(f32[1024,768]{1,0:T(8,128)S(1)} %fusion.21), kind=kLoop, calls=%fused_computation.30 | loop fusion | flops 25952256 | bytes 5505024 | tf_op jit(solution)/shard_map/convert_element_type | solution.py:356
  177.9 0.9 copy-done.24
  178.8 2.6 convolution_convert_fusion.1
  181.5 1.0 copy-done.5
  183.2 1.3 div.106
  184.5 0.9 fusion.48
  186.1 2.1 multiply_convert_fusion.1
  188.2 4.3 copy.114
  192.4 2.5 copy.118
  195.0 5.2 %fusion.49 = (f32[1024,384]{1,0:T(8,128)S(1)}, f32[1024,384]{1,0:T(8,128)S(1)}) fusion(f32[1024,384]{1,0:T(8,128)} %get-tuple-element.17, f32[1024,768]{1,0:T(8,128)} %copy-done.12, bf16[1024,1024]{1,0:T(8,128)(2,1)} %all-gather.8.cloned.1.call-done, bf16[1024,1152]{1,0:T(8,128)(2,1)} %bitcast.185), kind=kOutput, calls=%fused_computation.95 | convolution fusion | flops 811597824 | bytes 10747904 | tf_op jit(solution)/shard_map/dot_general | solution.py:357
  200.2 1.8 convolution_convert_fusion.3
  202.0 31.5 %shard_map.149 = f32[128,1024]{1,0:T(8,128)S(1)} custom-call(bf16[8,128,1024]{2,1,0:T(8,128)(2,1)S(1)} %bitcast.170), custom_call_target="tpu_custom_call" | custom-call | tf_op jit(solution)/shard_map/pallas_call | solution.py:246
  233.5 1.3 convolution_convert_fusion.5
  235.1 1.8 convolution_convert_fusion.4
  237.2 1.7 copy.119
  239.9 2.0 fusion.71
  242.7 1.1 fusion.50
  244.8 0.9 copy.109
  245.6 13.2 %shard_map.150 = bf16[8,128,128]{2,1,0:T(8,128)(2,1)} custom-call(bf16[8,128,128]{2,1,0:T(8,128)(2,1)} %bitcast.201), custom_call_target="tpu_custom_call" | custom-call | tf_op jit(solution)/shard_map/pallas_call | solution.py:110
  258.9 1.2 copy.110
  260.2 5.0 %multiply_reduce_fusion = (f32[2,1024]{1,0:T(2,128)S(1)}, f32[2,1024,1024]{1,2,0:T(8,128)S(1)}) fusion(f32[2,1024,1024]{1,2,0:T(8,128)} %get-tuple-element.44, f32[2,1024]{1,0:T(2,128)S(1)} %copy-done.39, bf16[1024,2,192]{0,2,1:T(8,128)(2,1)} %bitcast.208, bf16[1024,2,64]{0,2,1:T(8,128)(2,1)S(1)} %reshape.318), kind=kOutput, calls=%fused_computation.2 | convolution fusion | flops 274724864 | bytes 17317888 | tf_op jit(solution)/shard_map/hqe,hke->hqk/dot_general | solution.py:386
  265.2 5.0 %multiply_convert_fusion = bf16[2,1024,1024]{1,2,0:T(8,128)(2,1)S(1)} fusion(f32[2,1024,1024]{1,2,0:T(8,128)S(1)} %get-tuple-element.48, f32[2,1024]{1,0:T(2,128)S(1)} %get-tuple-element.47, f32[2,1024,1024]{1,2,0:T(8,128)} %get-tuple-element.44, f32[2,1024]{1,0:T(2,128)S(1)} %copy-done.39), kind=kLoop, calls=%fused_computation.1 | loop fusion | flops 8388608 | bytes 20987904 | tf_op jit(solution)/shard_map/convert_element_type | solution.py:388
  270.2 0.8 fusion.30
  272.0 1.4 fusion.29
  274.4 2.1 convolution_convert_fusion.2
  276.5 5.0 %fusion.26 = bf16[1024,2,192]{0,2,1:T(8,128)(2,1)S(1)} fusion(bf16[1024,2,192]{0,2,1:T(8,128)(2,1)S(1)} %subtract_dynamic-update-slice_fusion, bf16[1024,2,64]{0,2,1:T(8,128)(2,1)S(1)} %reshape.318, f32[2,1024,1024]{1,2,0:T(8,128)} %get-tuple-element.44, f32[2,1024]{1,0:T(2,128)S(1)} %copy-done.39), kind=kOutput, calls=%fused_computation.53 | convolution fusion | flops 272629760 | bytes 9183232 | tf_op jit(solution)/shard_map/hqk,hqe->khe/dot_general | solution.py:385
  281.4 1.3 convolution_convert_fusion
  282.8 24.6 %shard_map.151 = f32[128,1024]{1,0:T(8,128)S(1)} custom-call(bf16[8,128,1024]{2,1,0:T(8,128)(2,1)S(1)} %bitcast.171), custom_call_target="tpu_custom_call" | custom-call | tf_op jit(solution)/shard_map/pallas_call | solution.py:246
  309.2 11.0 %shard_map.152 = bf16[2,2,64,1024]{3,2,1,0:T(8,128)(2,1)} custom-call(bf16[2,2,64,1024]{3,2,1,0:T(8,128)(2,1)} %maximum_bitcast_fusion.2.x_ref), custom_call_target="tpu_custom_call" | custom-call | tf_op jit(solution)/shard_map/pallas_call | solution.py:110
  320.5 1.3 convolution_convert_fusion.6
  321.9 1.1 copy.117
  323.0 21.4 %shard_map.153 = bf16[4,256,512]{2,1,0:T(8,128)(2,1)} custom-call(bf16[4,256,512]{2,1,0:T(8,128)(2,1)} %bitcast.179), custom_call_target="tpu_custom_call" | custom-call | tf_op jit(solution)/shard_map/pallas_call | solution.py:110
  344.4 1.5 reduce_sum.193
  345.9 0.9 bitcast_convert_fusion
  346.8 2.0 pad_maximum_fusion
  348.8 25.3 %shard_map.154 = bf16[8,32,1664]{2,1,0:T(8,128)(2,1)} custom-call(bf16[8,32,1664]{2,1,0:T(8,128)(2,1)} %bitcast.181), custom_call_target="tpu_custom_call" | custom-call | tf_op jit(solution)/shard_map/pallas_call | solution.py:110
  374.2 1.0 convert_bitcast_fusion.1
  375.4 0.9 reshape.329
  378.0 1.2 reshape.328
  379.9 43.9 %reduce-scatter.8.cloned.1.call-done = bf16[32,1024]{1,0:T(8,128)(2,1)} async-done(((bf16[1024,1024]{1,0:T(8,128)(2,1)}), bf16[32,1024]{1,0:T(8,128)(2,1)}) %reduce-scatter.8.cloned.1.call-update) | async-done | bytes 65552 | tf_op jit(solution)/shard_map/reduce_scatter | solution.py:378
  423.8 1.5 convert_element_type.215
  (179 shorter events, 19.6 us)
Async XLA Ops:
  7.2 131.0 %all-gather.4.cloned.1.call-start = ((), (), s32[]{:S(2)}) async-start(), calls=%async_computation.4 | async-start | bytes 2162688 | tf_op jit(solution)/shard_map/all_gather | solution.py:307
  7.9 161.5 %all-gather.6.cloned.1.call-start = ((), (), s32[]{:S(2)}) async-start(), calls=%async_computation.5 | async-start | bytes 2949120 | tf_op jit(solution)/shard_map/all_gather | solution.py:305
  11.8 24.7 %copy-start.35 = (bf16[2,64,1024]{2,1,0:T(8,128)(2,1)S(1)}, bf16[2,64,1024]{2,1,0:T(8,128)(2,1)}, u32[]{:S(2)}) copy-start(bf16[2,64,1024]{2,1,0:T(8,128)(2,1)} %param.15) | copy-start | bytes 786436
  11.9 24.7 %copy-start.36 = (bf16[2,64,1024]{2,1,0:T(8,128)(2,1)S(1)}, bf16[2,64,1024]{2,1,0:T(8,128)(2,1)}, u32[]{:S(2)}) copy-start(bf16[2,64,1024]{2,1,0:T(8,128)(2,1)} %param.8) | copy-start | bytes 786436
  36.5 158.5 %all-gather.8.cloned.1.call-start = ((), (), s32[]{:S(2)}) async-start(), calls=%async_computation.7 | async-start | bytes 2359296 | tf_op jit(solution)/shard_map/all_gather | solution.py:325
  36.5 13.4 %copy-start.49 = (bf16[32]{0:T(256)(128)(2,1)S(1)}, bf16[32]{0:T(256)(128)(2,1)}, u32[]{:S(2)}) copy-start(bf16[32]{0:T(256)(128)(2,1)} %param.12) | copy-start | bytes 196
  36.5 13.4 %copy-start.50 = (bf16[32]{0:T(256)(128)(2,1)S(1)}, bf16[32]{0:T(256)(128)(2,1)}, u32[]{:S(2)}) copy-start(bf16[32]{0:T(256)(128)(2,1)} %param.9) | copy-start | bytes 196
  36.5 13.5 %copy-start.37 = (bf16[32,3072]{1,0:T(8,128)(2,1)S(1)}, bf16[32,3072]{1,0:T(8,128)(2,1)}, u32[]{:S(2)}) copy-start(bf16[32,3072]{1,0:T(8,128)(2,1)} %param.10) | copy-start | bytes 589828
  49.9 190.0 %reduce-scatter.4.cloned.1.call-start = ((), (), s32[]{:S(2)}) async-start(), calls=%async_computation.6 | async-start | bytes 2359296 | tf_op jit(solution)/shard_map/reduce_scatter | solution.py:362
  59.6 49.7 %copy-start.8 = (f32[1024,32]{0,1:T(8,128)}, f32[1024,32]{0,1:T(8,128)S(1)}, u32[]{:S(2)}) copy-start(f32[1024,32]{0,1:T(8,128)S(1)} %get-tuple-element.42) | copy-start | bytes 393220
  78.9 1.0 copy-start.15
  104.0 2.2 copy-start
  106.9 1.2 copy-start.16
  109.2 0.9 copy-start.34
  110.1 5.1 %copy-start.26 = (bf16[1024,2,32]{0,2,1:T(8,128)(2,1)}, bf16[1024,2,32]{0,2,1:T(8,128)(2,1)S(1)}, u32[]{:S(2)}) copy-start(bf16[1024,2,32]{0,2,1:T(8,128)(2,1)S(1)} %get-tuple-element.22) | copy-start | bytes 393220
  110.1 5.1 %copy-start.28 = (bf16[1024,2,32]{0,2,1:T(8,128)(2,1)}, bf16[1024,2,32]{0,2,1:T(8,128)(2,1)S(1)}, u32[]{:S(2)}) copy-start(bf16[1024,2,32]{0,2,1:T(8,128)(2,1)S(1)} %get-tuple-element.23) | copy-start | bytes 393220
  110.1 5.1 %copy-start.30 = (bf16[1024,2,32]{0,2,1:T(8,128)(2,1)}, bf16[1024,2,32]{0,2,1:T(8,128)(2,1)S(1)}, u32[]{:S(2)}) copy-start(bf16[1024,2,32]{0,2,1:T(8,128)(2,1)S(1)} %get-tuple-element.33) | copy-start | bytes 393220
  110.1 5.1 %copy-start.32 = (bf16[1024,2,32]{0,2,1:T(8,128)(2,1)}, bf16[1024,2,32]{0,2,1:T(8,128)(2,1)S(1)}, u32[]{:S(2)}) copy-start(bf16[1024,2,32]{0,2,1:T(8,128)(2,1)S(1)} %get-tuple-element.34) | copy-start | bytes 393220
  115.2 4.4 %copy-start.38 = (f32[2,1024]{1,0:T(2,128)}, f32[2,1024]{1,0:T(2,128)S(1)}, u32[]{:S(2)}) copy-start(f32[2,1024]{1,0:T(2,128)S(1)} %get-tuple-element.43) | copy-start | bytes 24580
  119.6 18.6 %copy-start.1 = (bf16[2,1,64,1024]{3,2,1,0:T(8,128)(2,1)S(1)}, bf16[2,1,64,1024]{3,2,1,0:T(8,128)(2,1)}, u32[]{:S(2)}) copy-start(bf16[2,1,64,1024]{3,2,1,0:T(8,128)(2,1)} %get-tuple-element.32) | copy-start | bytes 786436
  138.1 2.3 copy-start.18
  140.4 29.0 %copy-start.40 = (f32[128]{0:T(128)}, f32[128]{0:T(128)S(1)}, u32[]{:S(2)}) copy-start(f32[128]{0:T(128)S(1)} %broadcast_multiply_fusion.2) | copy-start | bytes 1540
  140.6 28.8 %copy-start.46 = (f32[128]{0:T(128)}, f32[128]{0:T(128)S(1)}, u32[]{:S(2)}) copy-start(f32[128]{0:T(128)S(1)} %multiply_reduce_fusion.5) | copy-start | bytes 1540
  140.6 28.8 %copy-start.43 = (f32[128]{0:T(128)}, f32[128]{0:T(128)S(1)}, u32[]{:S(2)}) copy-start(f32[128]{0:T(128)S(1)} %fusion.57) | copy-start | bytes 1540
  169.4 2.3 copy-start.3
  171.5 6.4 %copy-start.13 = (bf16[2,8,2,32,1152]{4,3,2,1,0:T(8,128)(2,1)}, bf16[2,8,2,32,1152]{4,3,2,1,0:T(8,128)(2,1)S(1)}, u32[]{:S(2)}) copy-start(bf16[2,8,2,32,1152]{4,3,2,1,0:T(8,128)(2,1)S(1)} %copy.107) | copy-start | bytes 7077892
  173.5 4.4 %copy-start.12 = (f32[1024,768]{1,0:T(8,128)}, f32[1024,768]{1,0:T(8,128)S(1)}, u32[]{:S(2)}) copy-start(f32[1024,768]{1,0:T(8,128)S(1)} %fusion.21) | copy-start | bytes 9437188
  177.9 0.9 copy-start.24
  181.4 1.0 copy-start.5
  181.5 165.3 %reduce-scatter.6.cloned.1.call-start = ((), (), s32[]{:S(2)}) async-start(), calls=%async_computation.8 | async-start | bytes 2949120 | tf_op jit(solution)/shard_map/reduce_scatter | solution.py:366
  188.2 4.3 copy-start.4
  195.0 5.2 %copy-start.14 = (bf16[2,8,2,32,1152]{4,3,2,1,0:T(8,128)(2,1)S(1)}, bf16[2,8,2,32,1152]{4,3,2,1,0:T(8,128)(2,1)}, u32[]{:S(2)}) copy-start(bf16[2,8,2,32,1152]{4,3,2,1,0:T(8,128)(2,1)} %copy-done.13) | copy-start | bytes 7077892
  200.2 33.3 %copy-start.48 = (bf16[1024,1024]{1,0:T(8,128)(2,1)S(1)}, bf16[1024,1024]{1,0:T(8,128)(2,1)}, u32[]{:S(2)}) copy-start(bf16[1024,1024]{1,0:T(8,128)(2,1)} %all-gather.8.cloned.1.call-done) | copy-start | bytes 6291460
  202.0 31.5 %copy-start.25 = (bf16[1024,384]{1,0:T(8,128)(2,1)S(1)}, bf16[1024,384]{1,0:T(8,128)(2,1)}, u32[]{:S(2)}) copy-start(bf16[1024,384]{1,0:T(8,128)(2,1)} %copy-done.24) | copy-start | bytes 2359300
  233.5 1.6 copy-start.21
  237.2 1.8 copy-start.41
  237.2 1.7 copy-start.44
  237.2 2.0 copy-start.47
  239.8 4.0 copy-start.2
  239.8 184.0 %reduce-scatter.8.cloned.1.call-start = ((), (), s32[]{:S(2)}) async-start(), calls=%async_computation.9 | async-start | bytes 2162688 | tf_op jit(solution)/shard_map/reduce_scatter | solution.py:378
  241.9 0.8 copy-start.6
  244.6 15.5 %copy-start.39 = (f32[2,1024]{1,0:T(2,128)S(1)}, f32[2,1024]{1,0:T(2,128)}, u32[]{:S(2)}) copy-start(f32[2,1024]{1,0:T(2,128)} %copy-done.38) | copy-start | bytes 24580
  265.2 5.0 %copy-start.31 = (bf16[1024,2,32]{0,2,1:T(8,128)(2,1)S(1)}, bf16[1024,2,32]{0,2,1:T(8,128)(2,1)}, u32[]{:S(2)}) copy-start(bf16[1024,2,32]{0,2,1:T(8,128)(2,1)} %copy-done.30) | copy-start | bytes 393220
  265.2 5.0 %copy-start.33 = (bf16[1024,2,32]{0,2,1:T(8,128)(2,1)S(1)}, bf16[1024,2,32]{0,2,1:T(8,128)(2,1)}, u32[]{:S(2)}) copy-start(bf16[1024,2,32]{0,2,1:T(8,128)(2,1)} %copy-done.32) | copy-start | bytes 393220
  270.2 0.9 copy-start.9
  271.1 0.9 copy-start.27
  271.1 1.0 copy-start.29
  273.4 1.0 copy-start.19
  276.5 5.0 %copy-start.17 = (bf16[2,2,8,32,512]{4,3,1,2,0:T(8,128)(2,1)S(1)}, bf16[2,2,8,32,512]{4,3,1,2,0:T(8,128)(2,1)}, u32[]{:S(2)}) copy-start(bf16[2,2,8,32,512]{4,3,1,2,0:T(8,128)(2,1)} %copy-done.15) | copy-start | bytes 3145732
  282.8 24.6 %copy-start.42 = (f32[128]{0:T(128)S(1)}, f32[128]{0:T(128)}, u32[]{:S(2)}) copy-start(f32[128]{0:T(128)} %div.106) | copy-start | bytes 1540
  282.8 24.9 %copy-start.45 = (f32[128]{0:T(128)S(1)}, f32[128]{0:T(128)}, u32[]{:S(2)}) copy-start(f32[128]{0:T(128)} %add.90) | copy-start | bytes 1540
  282.8 25.2 %copy-start.7 = (f32[128,1024]{1,0:T(8,128)S(1)}, f32[128,1024]{1,0:T(8,128)}, u32[]{:S(2)}) copy-start(f32[128,1024]{1,0:T(8,128)} %copy-done.6) | copy-start | bytes 1572868
  282.8 25.2 %copy-start.10 = (bf16[2,1,64,1024]{3,2,1,0:T(8,128)(2,1)S(1)}, bf16[2,1,64,1024]{3,2,1,0:T(8,128)(2,1)}, u32[]{:S(2)}) copy-start(bf16[2,1,64,1024]{3,2,1,0:T(8,128)(2,1)} %get-tuple-element.31) | copy-start | bytes 786436
  307.4 1.0 copy-start.23
  308.3 12.2 %copy-start.20 = (bf16[1024,1024]{1,0:T(8,128)(2,1)S(1)}, bf16[1024,1024]{1,0:T(8,128)(2,1)}, u32[]{:S(2)}) copy-start(bf16[1024,1024]{1,0:T(8,128)(2,1)} %copy.114) | copy-start | bytes 6291460
  323.0 22.9 %copy-start.22 = (bf16[2,2,64,1024]{3,2,1,0:T(8,128)(2,1)S(1)}, bf16[2,2,64,1024]{3,2,1,0:T(8,128)(2,1)}, u32[]{:S(2)}) copy-start(bf16[2,2,64,1024]{3,2,1,0:T(8,128)(2,1)} %shard_map.152) | copy-start | bytes 1572868
  374.1 2.2 copy-start.11
  375.2 2.0 slice-start
Sparse Core Ops, SparseCore 0:
  10.9 62.2 all-gather.3
  75.1 36.3 all-gather.5
  113.7 35.2 all-gather.7
  181.6 43.0 reduce-scatter.3
  239.9 41.9 reduce-scatter.5
  284.0 139.7 reduce-scatter.7

commit v2 on v1

--- a/solution.py
+++ b/solution.py
@@ -66,128 +66,106 @@
 MESH = pl.DeviceIdType.MESH
 
 
-def exchange(x, axes, cid):
-    sizes = [lax.axis_size(a) for a in axes]
-    n = math.prod(sizes)
-
-    def kernel(x_ref, o_ref, send, recv, local):
-        me = 0
-        for a, s in zip(axes, sizes):
-            me = me * s + lax.axis_index(a)
-
-        def place(k):
-            ids = {}
-            for a, s in reversed(list(zip(axes, sizes))):
-                ids[a] = lax.rem(k, s)
-                k = k // s
-            return ids
-
+def together(ops, cid):
+    n_u = lax.axis_size("ulysses")
+    counts = []
+    shapes = []
+    for kind, x, axes in ops:
+        n = n_u if kind == "line" else math.prod(lax.axis_size(a) for a in axes)
+        counts.append(n)
+        shape = x.shape if kind == "swap" else (n,) + x.shape
+        shapes.append(jax.ShapeDtypeStruct(shape, x.dtype))
+    many = len(ops)
+
+    def kernel(*refs):
+        sources, results, sems = refs[:many], refs[many : 2 * many], refs[2 * many :]
         barrier = pltpu.get_barrier_semaphore()
-        for k in range(1, n):
-            pl.semaphore_signal(
-                barrier, 1, device_id=place(lax.rem(me + k, n)), device_id_type=MESH
-            )
-        pl.semaphore_wait(barrier, n - 1)
-        copies = []
-        for k in range(1, n):
-            peer = lax.rem(me + k, n)
+        plans = []
+        expected = 0
+        for (kind, _, axes), n in zip(ops, counts):
+            if kind == "line":
+                me = lax.axis_index("ulysses")
+                chip, core = me // 2, lax.rem(me, 2)
+                peers = [chip * 2 + (1 - core)]
+                peers += [lax.rem(chip + k, n // 2) * 2 + core for k in range(1, n // 2)]
+                places = [{"ulysses": peer} for peer in peers]
+            else:
+                me = 0
+                for a in axes:
+                    me = me * lax.axis_size(a) + lax.axis_index(a)
+                peers = [lax.rem(me + k, n) for k in range(1, n)]
+                places = []
+                for peer in peers:
+                    ids = {}
+                    for a in reversed(axes):
+                        ids[a] = lax.rem(peer, lax.axis_size(a))
+                        peer = peer // lax.axis_size(a)
+                    places.append(ids)
+            for ids in places:
+                pl.semaphore_signal(barrier, 1, device_id=ids, device_id_type=MESH)
+            expected += len(places)
+            plans.append((me, peers, places))
+        pl.semaphore_wait(barrier, expected)
+
+        def remote(source, target, send, recv, ids):
             copy = pltpu.make_async_remote_copy(
-                src_ref=x_ref.at[peer],
-                dst_ref=o_ref.at[me],
-                send_sem=send.at[k],
-                recv_sem=recv.at[k],
-                device_id=place(peer),
+                src_ref=source,
+                dst_ref=target,
+                send_sem=send,
+                recv_sem=recv,
+                device_id=ids,
                 device_id_type=MESH,
             )
             copy.start()
-            copies.append(copy)
-        own = pltpu.make_async_copy(x_ref.at[me], o_ref.at[me], local)
-        own.start()
-        own.wait()
-        for copy in copies:
+            return copy
+
+        started, local = [], []
+        for i, (kind, _, _) in enumerate(ops):
+            me, peers, places = plans[i]
+            source, result = sources[i], results[i]
+            send, recv, own = sems[3 * i : 3 * i + 3]
+            copies = []
+            for j in range(len(peers)):
+                part = source.at[peers[j]] if kind == "swap" else source
+                copies.append(remote(part, result.at[me], send.at[j], recv.at[j], places[j]))
+            started.append(copies)
+            part = source.at[me] if kind == "swap" else source
+            local.append(pltpu.make_async_copy(part, result.at[me], own))
+            local[-1].start()
+        passed = []
+        for i, (kind, _, _) in enumerate(ops):
+            if kind != "line":
+                continue
+            me, _, places = plans[i]
+            chips = counts[i] // 2
+            chip, core = me // 2, lax.rem(me, 2)
+            send, recv, _ = sems[3 * i : 3 * i + 3]
+            for k in range(1, chips):
+                started[i][k].wait_recv()
+                slot = results[i].at[lax.rem(chip - k + chips, chips) * 2 + core]
+                at = chips + k - 1
+                passed.append(remote(slot, slot, send.at[at], recv.at[at], places[0]))
+        for i, (kind, _, _) in enumerate(ops):
+            for j, copy in enumerate(started[i]):
+                if kind == "line" and j:
+                    copy.wait_send()
+                else:
+                    copy.wait()
+            local[i].wait()
+        for copy in passed:
             copy.wait()
 
+    scratch = []
+    for n in counts:
+        scratch += [pltpu.SemaphoreType.DMA((n,))] * 2 + [pltpu.SemaphoreType.DMA]
     return pl.pallas_call(
         kernel,
-        out_shape=jax.ShapeDtypeStruct(x.shape, x.dtype),
-        in_specs=[pl.BlockSpec(memory_space=pl.ANY)],
-        out_specs=pl.BlockSpec(memory_space=pl.ANY),
-        scratch_shapes=[
-            pltpu.SemaphoreType.DMA((n,)),
-            pltpu.SemaphoreType.DMA((n,)),
-            pltpu.SemaphoreType.DMA,
-        ],
+        out_shape=shapes,
+        in_specs=[pl.BlockSpec(memory_space=pl.ANY)] * many,
+        out_specs=[pl.BlockSpec(memory_space=pl.ANY)] * many,
+        scratch_shapes=scratch,
         compiler_params=pltpu.CompilerParams(collective_id=cid, has_side_effects=True),
-    )(x)
-
-
-def gather_line(x, cid):
-    n = lax.axis_size("ulysses")
-    chips = n // 2
-
-    def kernel(x_ref, o_ref, send, recv, pass_send, pass_recv, local):
-        me = lax.axis_index("ulysses")
-        chip, core = me // 2, lax.rem(me, 2)
-        partner = chip * 2 + (1 - core)
-        barrier = pltpu.get_barrier_semaphore()
-        pl.semaphore_signal(barrier, 1, device_id={"ulysses": partner}, device_id_type=MESH)
-        for k in range(1, chips):
-            peer = lax.rem(chip + k, chips) * 2 + core
-            pl.semaphore_signal(barrier, 1, device_id={"ulysses": peer}, device_id_type=MESH)
-        pl.semaphore_wait(barrier, chips)
-        far = []
-        for k in range(1, chips):
-            peer = lax.rem(chip + k, chips) * 2 + core
-            copy = pltpu.make_async_remote_copy(
-                src_ref=x_ref,
-                dst_ref=o_ref.at[me],
-                send_sem=send.at[k],
-                recv_sem=recv.at[k],
-                device_id={"ulysses": peer},
-                device_id_type=MESH,
-            )
-            copy.start()
-            far.append(copy)
-        near = [
-            pltpu.make_async_remote_copy(
-                src_ref=x_ref,
-                dst_ref=o_ref.at[me],
-                send_sem=pass_send.at[0],
-                recv_sem=pass_recv.at[0],
-                device_id={"ulysses": partner},
-                device_id_type=MESH,
-            )
-        ]
-        near[0].start()
-        own = pltpu.make_async_copy(x_ref, o_ref.at[me], local)
-        own.start()
-        for k in range(1, chips):
-            far[k - 1].wait_recv()
-            slot = lax.rem(chip - k + chips, chips) * 2 + core
-            copy = pltpu.make_async_remote_copy(
-                src_ref=o_ref.at[slot],
-                dst_ref=o_ref.at[slot],
-                send_sem=pass_send.at[k],
-                recv_sem=pass_recv.at[k],
-                device_id={"ulysses": partner},
-                device_id_type=MESH,
-            )
-            copy.start()
-            near.append(copy)
-        own.wait()
-        for copy in far:
-            copy.wait_send()
-        for copy in near:
-            copy.wait()
-
-    return pl.pallas_call(
-        kernel,
-        out_shape=jax.ShapeDtypeStruct((n,) + x.shape, x.dtype),
-        in_specs=[pl.BlockSpec(memory_space=pl.ANY)],
-        out_specs=pl.BlockSpec(memory_space=pl.ANY),
-        scratch_shapes=[pltpu.SemaphoreType.DMA((chips,))] * 4 + [pltpu.SemaphoreType.DMA],
-        compiler_params=pltpu.CompilerParams(collective_id=cid, has_side_effects=True),
-    )(x)
+    )(*[x for _, x, _ in ops])
 
 
 def scatter_line(x, cid):
@@ -299,29 +277,38 @@
         grads = grads.reshape(n_dp, n_u, n_b, part, cols).transpose(0, 2, 1, 3, 4)
         return grads.reshape(n_dp * n_b, n_u * part, cols)
 
-    first_cut = exchange(first_cut, ("ulysses",), 1)
-    mlp_cut = lax.all_to_all(mlp_cut, "ulysses", 0, 0)
+    both, first_cut, mlp_cut = together(
+        [
+            ("swap", jnp.stack([tokens, cotangent], axis=1), ("blk",)),
+            ("swap", first_cut, ("ulysses",)),
+            ("swap", mlp_cut, ("ulysses",)),
+        ],
+        1,
+    )
+    inputs_low = both[:, 0].reshape(rows, width)
+    grad_top = both[:, 1].reshape(rows, width)
+    first_full, tokens_all = together(
+        [
+            ("copy", first_cut.reshape(n_u * part, -1), ("dp", "blk")),
+            ("line", inputs_low, None),
+        ],
+        2,
+    )
     mlp_full = in_order(
         lax.all_gather(mlp_cut.reshape(n_u * part, -1), ("dp", "blk"), axis=0, tiled=True)
     )
     out_full = lax.all_gather(
         attention_output_weight, ("dp", "ulysses", "blk"), axis=0, tiled=True
     )
-    copies = jnp.broadcast_to(
-        first_cut.reshape(1, n_u * part, -1), (n_dp * n_b, n_u * part, head_cols + 128)
-    )
-    first_full = in_order(exchange(copies, ("dp", "blk"), 2))
+    first_full = in_order(first_full)
     qkv_w = first_full[:, :head_cols]
     gain_attn_f = first_full[:, head_cols].astype(f32)
     gain_mlp_f = first_full[:, head_cols + 1].astype(f32)
     in_w = mlp_full[:, : 2 * ff_pad]
     down_w = mlp_full[:, 2 * ff_pad :]
 
-    both = exchange(jnp.stack([tokens, cotangent], axis=1), ("blk",), 3)
-    inputs_low = both[:, 0].reshape(rows, width)
-    grad_top = both[:, 1].reshape(rows, width)
     inputs = inputs_low.astype(f32)
-    tokens_all = gather_line(inputs_low, 4).reshape(length, width)
+    tokens_all = tokens_all.reshape(length, width)
     cot_all = lax.all_gather(grad_top, "ulysses", axis=0, tiled=True)
     normed = layer_norm(tokens_all.astype(f32), gain_attn_f).astype(BF)
     joined = jnp.dot(normed, qkv_w, preferred_element_type=f32).astype(BF)
@@ -342,11 +329,13 @@
     probs = weights.astype(BF)
     attended = jnp.einsum("hqk,hke->qhe", probs, values, preferred_element_type=f32)
     attended = attended.astype(BF).reshape(n_u, rows, heads * HEAD_DIM)
-    back = exchange(attended, ("ulysses",), 5).transpose(1, 0, 2).reshape(rows, width)
+    (back,) = together([("swap", attended, ("ulysses",))], 5)
+    back = back.transpose(1, 0, 2).reshape(rows, width)
 
     middle = inputs + jnp.dot(back, out_full, preferred_element_type=f32)
     normed_mlp_own = layer_norm(middle, gain_mlp_f).astype(BF)
-    normed_mlp = gather_line(normed_mlp_own, 6).reshape(length, width)
+    (normed_mlp,) = together([("line", normed_mlp_own, None)], 6)
+    normed_mlp = normed_mlp.reshape(length, width)
     hidden = jnp.dot(normed_mlp, in_w, preferred_element_type=f32)
 
     def gated(hidden):
@@ -373,14 +362,11 @@
     grad_branch = grad_middle.astype(BF)
     grad_back = contract_cols(grad_branch, out_full).astype(BF)
     grad_back = grad_back.reshape(rows, n_u, heads * HEAD_DIM).transpose(1, 0, 2)
-    grad_heads = exchange(grad_back, ("ulysses",), 8).reshape(length, heads, HEAD_DIM)
-    grad_heads = grad_heads.transpose(1, 0, 2)
-    grad_out = lax.psum_scatter(
-        contract_rows(back, grad_branch).astype(BF),
-        ("dp", "ulysses", "blk"),
-        scatter_dimension=0,
-        tiled=True,
-    ).astype(f32)
+    (grad_heads,) = together([("swap", grad_back, ("ulysses",))], 8)
+    grad_heads = grad_heads.reshape(length, heads, HEAD_DIM).transpose(1, 0, 2)
+    branch_all = lax.all_gather(grad_branch, "ulysses", axis=0, tiled=True)
+    grad_out = contract_rows(attended.reshape(length, heads * HEAD_DIM), branch_all)
+    grad_out = grad_out.astype(BF).reshape(n_dp * n_b, part, width)
 
     grad_values = jnp.einsum("hqk,hqe->khe", probs, grad_heads, preferred_element_type=f32)
     grad_probs = jnp.einsum("hqe,hke->hqk", grad_heads, values, preferred_element_type=f32)
@@ -401,21 +387,33 @@
     output = middle + mlp_sum.astype(f32)
     ends = jnp.stack([output.astype(BF), input_grad.astype(BF)], axis=0)
     ends = ends.reshape(2, seq_count, local_len, width).transpose(1, 0, 2, 3)
-    ends = exchange(ends, ("blk",), 10)
-    output, input_grad = ends[:, 0], ends[:, 1].astype(f32)
-
     gain_parts = pad_to(jnp.stack([gain_attn_part, gain_mlp_part], axis=1), 128)
     first_grads = jnp.concatenate([contract_rows(normed, grad_joined), gain_parts], axis=1)
-    first_grads = exchange(by_owner(first_grads.astype(BF)), ("dp", "blk"), 11)
+    ends, first_grads, grad_out, last_mlp = together(
+        [
+            ("swap", ends, ("blk",)),
+            ("swap", by_owner(first_grads.astype(BF)), ("dp", "blk")),
+            ("swap", grad_out, ("dp", "blk")),
+            ("swap", mlp_grads.reshape(n_u, part, -1), ("ulysses",)),
+        ],
+        10,
+    )
+    output, input_grad = ends[:, 0], ends[:, 1].astype(f32)
+    owners = [
+        ((d * n_u + u) * n_b + b, u * n_dp * n_b + d * n_b + b)
+        for d in range(n_dp)
+        for u in range(n_u)
+        for b in range(n_b)
+    ]
+    grad_out = jnp.sum(grad_out.astype(f32), axis=0).astype(BF)
+    grad_out = lax.ppermute(grad_out, ("dp", "ulysses", "blk"), owners).astype(f32)
     first_grads = jnp.sum(first_grads.astype(f32), axis=0).astype(BF)
-    last = jnp.concatenate([first_grads, mlp_grads], axis=1).reshape(n_u, part, -1)
-    last = exchange(last, ("ulysses",), 12)
+    (last,) = together([("swap", first_grads.reshape(n_u, part, -1), ("ulysses",))], 12)
     gain_sums = jnp.sum(last[:, :, head_cols : head_cols + 2].astype(f32), axis=0)
     grad_qkv = last[:, :, :head_cols].transpose(1, 0, 2).reshape(part, -1).astype(f32)
-    at = head_cols + 128
-    grad_in = last[:, :, at : at + 2 * ff_pad].reshape(n_u, part, 2, ff_pad)[..., :ff_cols]
+    grad_in = last_mlp[:, :, : 2 * ff_pad].reshape(n_u, part, 2, ff_pad)[..., :ff_cols]
     grad_in = grad_in.transpose(1, 2, 0, 3).reshape(part, -1).astype(f32)
-    grad_down = last[:, :, at + 2 * ff_pad :][..., :ff_cols]
+    grad_down = last_mlp[:, :, 2 * ff_pad :][..., :ff_cols]
     grad_down = grad_down.transpose(1, 0, 2).reshape(part, -1).astype(f32)
     return (
         output,

time: 439 us -> 407 us (0.927)
  blocking collectives: 24.5 us -> 0 us
  Pallas kernels: 230 us -> 216 us
  matrix products: 44.8 us -> 49.9 us
    reduce_scatter x1 -> x0, waiting for transfers between devices: 43.9 us -> none  [body(): lax.psum_scatter(contract_rows(back, grad_branch).astype(BF), ('dp', 'uly...]
    all_gather x1, waiting for transfers between devices: 0.02 us -> 41.6 us  [body(): lax.all_gather(attention_output_weight, ('dp', 'ulysses', 'blk'), axis=0,...]
    all_to_all x1 -> x0, blocking collectives: 24.5 us -> none  [body(): mlp_cut = lax.all_to_all(mlp_cut, 'ulysses', 0, 0)]
    pallas_call x10 -> x7, Pallas kernels: 174 us -> 149 us  [together(): pl.pallas_call(kernel, out_shape=shapes, in_specs=[pl.BlockSpec(memory_sp...]
    pallas_call x2, Pallas kernels: 56 us -> 67 us  [scatter_line(): pl.pallas_call(kernel, out_shape=jax.ShapeDtypeStruct((rows, cols), jnp.f...]
    reduce_scatter x1, waiting for transfers between devices: 0.02 us -> 6.69 us  [body(): lax.psum_scatter(mlp_part, 'ulysses', scatter_dimension=0, tiled=True)]
  transfers between devices with their start and end apart: 6 -> 7, of which waited for: 1 -> 2; matrix products, arithmetic and copies ran while one was open for 25% -> 24% of each run, Pallas kernels for 53% -> 39%
where the time goes in v2:
time: 407 us; the launch traced here: 401 us
  Pallas kernels  216 us (53%)
  matrix products  49.9 us (12%)
  waiting for transfers between devices  49.1 us (12%)
  local copies, waits for them, and re-layouts  35.3 us (9%)
  other arithmetic  33.2 us (8%)
  between operations  15.4 us (4%)
    pallas_call x7, Pallas kernels, together(): pl.pallas_call(kernel, out_shape=shapes, in_specs=[pl.BlockSpec(memory_sp...  149 us
    pallas_call x2, Pallas kernels, scatter_line(): pl.pallas_call(kernel, out_shape=jax.ShapeDtypeStruct((rows, cols), jnp.f...  67 us
    all_gather x1, waiting for transfers between devices, body(): lax.all_gather(attention_output_weight, ('dp', 'ulysses', 'blk'), axis=0,...  41.6 us
    dot_general x4, matrix products, contract_rows(): lax.dot_general(left_side, right_side, (((0,), (0,)), ((), ())), preferre...  10.2 us
  transfers between devices with their start and end apart: 7, of which 2 were waited for; matrix products, arithmetic and copies ran while one was open for 24% of the time, Pallas kernels for 39%

profile of v2, /device:TPU:0, one launch (start us, length us, event | category | flops | bytes accessed | tf_op | source)
XLA Modules:
  0.0 400.7 jit_solution(11039228787265183049)
XLA Ops:
  8.0 0.9 copy.137
  9.0 1.2 reshape.313
  12.7 0.9 pad_maximum_fusion.refs_2_
  13.6 0.8 pad_maximum_fusion.1.refs_0_
  14.4 21.2 %shard_map.143 = (bf16[2,2,64,1024]{3,2,1,0:T(8,128)(2,1)}, bf16[8,32,512]{2,1,0:T(8,128)(2,1)}, bf16[8,32,1152]{2,1,0:T(8,128)(2,1)}) custom-call(bf16[2,2,64,1024]{3,2,1,0:T(8,128)(2,1)} %pad_maximum_fusion.1.refs_0_, bf16[8,32,512]{2,1,0:T(8,128)(2,1)} %pad_maximum_fusion.2.refs_1_, bf16[8,32,1152]{2,1,0:T(8,128)(2,1)} %pad_maximum_fusion.refs_2_), custom_call_target="tpu_custom_call" | custom-call | tf_op jit(solution)/shard_map/pallas_call | solution.py:161
  36.4 1.9 fusion.72
  39.5 27.3 %shard_map.144 = (bf16[4,256,512]{2,1,0:T(8,128)(2,1)}, bf16[8,128,1024]{2,1,0:T(8,128)(2,1)}) custom-call(bf16[256,512]{1,0:T(8,128)(2,1)} %bitcast.217, bf16[128,1024]{1,0:T(8,128)(2,1)} %bitcast.177), custom_call_target="tpu_custom_call" | custom-call | tf_op jit(solution)/shard_map/pallas_call | solution.py:161
  66.7 1.4 copy.104
  70.7 1.0 convolution_convert_fusion.6
  71.9 0.9 subtract_convert_fusion.1
  72.8 7.0 %fusion.73 = (f32[2,1024]{1,0:T(2,128)S(1)}, f32[2,1024,1024]{1,2,0:T(8,128)}) fusion(bf16[1024,2,32]{0,2,1:T(8,128)(2,1)} %get-tuple-element.51, bf16[1024,2,32]{0,2,1:T(8,128)(2,1)} %get-tuple-element.52, bf16[1024,2,32]{0,2,1:T(8,128)(2,1)} %get-tuple-element.41, bf16[1024,2,32]{0,2,1:T(8,128)(2,1)S(1)} %get-tuple-element.40), kind=kOutput, calls=%fused_computation.153 | convolution fusion | flops 275776512 | bytes 8921088 | tf_op jit(solution)/shard_map/sub | solution.py:325
  79.9 4.3 %fusion.31 = bf16[2,64,1024]{2,1,0:T(8,128)(2,1)S(1)} fusion(bf16[1024,2,192]{0,2,1:T(8,128)(2,1)} %bitcast.215, f32[2,1024,1024]{1,2,0:T(8,128)} %get-tuple-element.62, f32[2,1024]{1,0:T(2,128)S(1)} %get-tuple-element.61), kind=kOutput, calls=%fused_computation.58 | convolution fusion | flops 272760832 | bytes 8921088 | tf_op jit(solution)/shard_map/hqk,hke->qhe/dot_general | solution.py:330
  84.3 0.9 copy.106.refs_0_
  85.2 13.6 %shard_map.145 = bf16[8,128,128]{2,1,0:T(8,128)(2,1)} custom-call(bf16[8,128,128]{2,1,0:T(8,128)(2,1)} %copy.106.refs_0_), custom_call_target="tpu_custom_call" | custom-call | tf_op jit(solution)/shard_map/pallas_call | solution.py:161
  98.8 1.1 copy.107
  99.9 3.4 copy.108
  103.3 41.6 %all-gather.5.cloned.1.call-done = bf16[1024,1024]{1,0:T(8,128)(2,1)} async-done(((bf16[32,1024]{1,0:T(8,128)(2,1)}), bf16[1024,1024]{1,0:T(8,128)(2,1)}) %all-gather.5.cloned.1.call-update) | async-done | bytes 2097168 | tf_op jit(solution)/shard_map/all_gather | solution.py:300
  144.9 2.1 fusion.74
  147.3 0.8 multiply_convert_fusion.3.refs_0_
  148.2 34.7 %shard_map.146 = bf16[8,128,1024]{2,1,0:T(8,128)(2,1)} custom-call(bf16[128,1024]{1,0:T(8,128)(2,1)} %multiply_convert_fusion.3.refs_0_), custom_call_target="tpu_custom_call" | custom-call | tf_op jit(solution)/shard_map/pallas_call | solution.py:161
  182.8 3.8 fusion.21
  186.7 4.5 %multiply_convert_fusion.2 = (bf16[1024,384]{1,0:T(8,128)(2,1)S(1)}, f32[1024,384]{1,0:T(8,128)}) fusion(f32[1024,768]{1,0:T(8,128)S(1)} %fusion.21), kind=kLoop, calls=%fused_computation.29 | loop fusion | flops 25952256 | bytes 5505024 | tf_op jit(solution)/shard_map/convert_element_type | solution.py:345
  191.2 0.9 copy-done.21
  192.1 3.7 convolution_convert_fusion.1
  196.0 5.1 %fusion.49 = (f32[1024,384]{1,0:T(8,128)S(1)}, f32[1024,384]{1,0:T(8,128)S(1)}) fusion(f32[1024,384]{1,0:T(8,128)} %get-tuple-element.35, f32[1024,768]{1,0:T(8,128)} %copy-done.10, bf16[1024,1024]{1,0:T(8,128)(2,1)} %all-gather.9.cloned.1.call-done, bf16[1024,1152]{1,0:T(8,128)(2,1)} %bitcast.189), kind=kOutput, calls=%fused_computation.94 | convolution fusion | flops 811597824 | bytes 10747904 | tf_op jit(solution)/shard_map/dot_general | solution.py:346
  201.1 1.8 convolution_convert_fusion.2
  203.0 41.6 %shard_map.147 = f32[128,1024]{1,0:T(8,128)S(1)} custom-call(bf16[8,128,1024]{2,1,0:T(8,128)(2,1)S(1)} %bitcast.174), custom_call_target="tpu_custom_call" | custom-call | tf_op jit(solution)/shard_map/pallas_call | solution.py:224
  244.6 0.8 multiply_reduce_fusion.3
  245.9 6.7 %reduce-scatter.3.cloned.1.call-done = bf16[128,1024]{1,0:T(8,128)(2,1)} async-done(((bf16[1024,1024]{1,0:T(8,128)(2,1)}), bf16[128,1024]{1,0:T(8,128)(2,1)}) %reduce-scatter.3.cloned.1.call-update) | async-done | bytes 262160 | tf_op jit(solution)/shard_map/reduce_scatter | solution.py:351
  252.6 1.9 fusion.71
  254.5 0.8 copy-done.4
  255.3 0.8 fusion.50
  256.2 1.1 convert_reduce_fusion.1
  257.7 2.0 multiply_convert_fusion.1
  259.7 4.2 %copy.115 = bf16[1024,1024]{1,0:T(8,128)(2,1)} copy(bf16[1024,1024]{0,1:T(8,128)(2,1)} %bitcast.179) | data formatting | bytes 4194304 | tf_op jit(solution)/shard_map/dot_general | solution.py:54
  263.9 2.5 copy.119
  266.5 3.2 convolution_convert_fusion.4
  270.1 1.8 convolution_convert_fusion.3
  272.2 1.7 copy.120
  274.0 1.6 copy-done.2
  275.5 0.8 convolution_convert_fusion.8
  276.5 0.9 copy.110
  277.4 14.9 %shard_map.148 = bf16[8,128,128]{2,1,0:T(8,128)(2,1)} custom-call(bf16[8,128,128]{2,1,0:T(8,128)(2,1)} %bitcast.205), custom_call_target="tpu_custom_call" | custom-call | tf_op jit(solution)/shard_map/pallas_call | solution.py:161
  292.3 1.1 copy.111
  293.6 4.9 %multiply_reduce_fusion = (f32[2,1024]{1,0:T(2,128)S(1)}, f32[2,1024,1024]{1,2,0:T(8,128)S(1)}) fusion(f32[2,1024,1024]{1,2,0:T(8,128)} %get-tuple-element.62, f32[2,1024]{1,0:T(2,128)S(1)} %copy-done.36, bf16[1024,2,192]{0,2,1:T(8,128)(2,1)} %bitcast.216, bf16[1024,2,64]{0,2,1:T(8,128)(2,1)S(1)} %reshape.326), kind=kOutput, calls=%fused_computation.2 | convolution fusion | flops 274724864 | bytes 17317888 | tf_op jit(solution)/shard_map/hqe,hke->hqk/dot_general | solution.py:372
  298.5 5.0 %multiply_convert_fusion = bf16[2,1024,1024]{1,2,0:T(8,128)(2,1)S(1)} fusion(f32[2,1024,1024]{1,2,0:T(8,128)S(1)} %get-tuple-element.66, f32[2,1024]{1,0:T(2,128)S(1)} %get-tuple-element.65, f32[2,1024,1024]{1,2,0:T(8,128)} %get-tuple-element.62, f32[2,1024]{1,0:T(2,128)S(1)} %copy-done.36), kind=kLoop, calls=%fused_computation.1 | loop fusion | flops 8388608 | bytes 20987904 | tf_op jit(solution)/shard_map/convert_element_type | solution.py:374
  303.6 0.8 fusion.30
  304.6 0.8 copy-done.24
  305.5 1.4 fusion.29
  307.0 1.4 fusion.26
  308.4 1.3 convolution_convert_fusion
  309.8 25.4 %shard_map.149 = f32[128,1024]{1,0:T(8,128)S(1)} custom-call(bf16[8,128,1024]{2,1,0:T(8,128)(2,1)S(1)} %bitcast.175), custom_call_target="tpu_custom_call" | custom-call | tf_op jit(solution)/shard_map/pallas_call | solution.py:224
  336.8 2.4 convolution_convert_fusion.5
  339.4 1.1 copy.118
  341.0 0.8 maximum_bitcast_fusion.2.refs_0_
  341.9 2.7 convolution_convert_fusion.7
  344.6 29.7 %shard_map.150 = (bf16[2,2,64,1024]{3,2,1,0:T(8,128)(2,1)}, bf16[4,256,512]{2,1,0:T(8,128)(2,1)}, bf16[4,32,1024]{2,1,0:T(8,128)(2,1)}, bf16[8,32,1152]{2,1,0:T(8,128)(2,1)}) custom-call(bf16[2,2,64,1024]{3,2,1,0:T(8,128)(2,1)} %maximum_bitcast_fusion.2.refs_0_, bf16[4,256,512]{2,1,0:T(8,128)(2,1)} %bitcast.184, bf16[4,32,1024]{2,1,0:T(8,128)(2,1)} %bitcast.196, ...), custom_call_target="tpu_custom_call" | custom-call | tf_op jit(solution)/shard_map/pallas_call | solution.py:161
  374.3 2.2 reduce_sum.205
  376.5 8.2 %shard_map.151 = bf16[8,32,512]{2,1,0:T(8,128)(2,1)} custom-call(bf16[8,32,512]{2,1,0:T(8,128)(2,1)} %bitcast.199), custom_call_target="tpu_custom_call" | custom-call | tf_op jit(solution)/shard_map/pallas_call | solution.py:161
  384.7 0.9 convert_reduce_fusion.4
  385.6 1.0 convert_bitcast_fusion.2
  388.1 0.9 bitcast_convert_fusion
  389.4 0.9 reshape.339
  391.0 1.2 reshape.338
  (174 shorter events, 16.8 us)
Async XLA Ops:
  7.2 3.1 copy-start.30
  7.2 92.7 %all-gather.7.cloned.1.call-start = ((), (), s32[]{:S(2)}) async-start(), calls=%async_computation.3 | async-start | bytes 2949120 | tf_op jit(solution)/shard_map/all_gather | solution.py:298
  11.3 2.3 copy-start.32
  11.3 2.3 copy-start.33
  35.6 109.3 %all-gather.5.cloned.1.call-start = ((), (), s32[]{:S(2)}) async-start(), calls=%async_computation.2 | async-start | bytes 2162688 | tf_op jit(solution)/shard_map/all_gather | solution.py:300
  36.4 159.6 %all-gather.9.cloned.1.call-start = ((), (), s32[]{:S(2)}) async-start(), calls=%async_computation.5 | async-start | bytes 2359296 | tf_op jit(solution)/shard_map/all_gather | solution.py:312
  38.3 214.3 %reduce-scatter.3.cloned.1.call-start = ((), (), s32[]{:S(2)}) async-start(), calls=%async_computation.4 | async-start | bytes 2359296 | tf_op jit(solution)/shard_map/reduce_scatter | solution.py:351
  39.4 32.5 %copy-start.6 = (f32[1024,32]{0,1:T(8,128)}, f32[1024,32]{0,1:T(8,128)S(1)}, u32[]{:S(2)}) copy-start(f32[1024,32]{0,1:T(8,128)S(1)} %get-tuple-element.60) | copy-start | bytes 393220
  66.7 1.9 copy-start
  68.2 2.5 copy-start.12
  71.8 1.1 copy-start.29
  72.8 7.0 %copy-start.23 = (bf16[1024,2,32]{0,2,1:T(8,128)(2,1)}, bf16[1024,2,32]{0,2,1:T(8,128)(2,1)S(1)}, u32[]{:S(2)}) copy-start(bf16[1024,2,32]{0,2,1:T(8,128)(2,1)S(1)} %get-tuple-element.40) | copy-start | bytes 393220
  79.9 4.3 %copy-start.35 = (f32[2,1024]{1,0:T(2,128)}, f32[2,1024]{1,0:T(2,128)S(1)}, u32[]{:S(2)}) copy-start(f32[2,1024]{1,0:T(2,128)S(1)} %get-tuple-element.61) | copy-start | bytes 24580
  84.2 19.1 %copy-start.18 = (bf16[2,64,1024]{2,1,0:T(8,128)(2,1)}, bf16[2,64,1024]{2,1,0:T(8,128)(2,1)S(1)}, u32[]{:S(2)}) copy-start(bf16[2,64,1024]{2,1,0:T(8,128)(2,1)S(1)} %fusion.31) | copy-start | bytes 786436
  99.9 45.0 %copy-start.1 = (bf16[2,1,64,1024]{3,2,1,0:T(8,128)(2,1)S(1)}, bf16[2,1,64,1024]{3,2,1,0:T(8,128)(2,1)}, u32[]{:S(2)}) copy-start(bf16[2,1,64,1024]{3,2,1,0:T(8,128)(2,1)} %get-tuple-element.50) | copy-start | bytes 786436
  147.1 35.8 %copy-start.38 = (f32[128]{0:T(128)}, f32[128]{0:T(128)S(1)}, u32[]{:S(2)}) copy-start(f32[128]{0:T(128)S(1)} %broadcast_multiply_fusion.2) | copy-start | bytes 1540
  147.3 35.6 %copy-start.42 = (f32[128]{0:T(128)}, f32[128]{0:T(128)S(1)}, u32[]{:S(2)}) copy-start(f32[128]{0:T(128)S(1)} %multiply_reduce_fusion.5) | copy-start | bytes 1540
  147.3 35.5 %copy-start.40 = (f32[128]{0:T(128)}, f32[128]{0:T(128)S(1)}, u32[]{:S(2)}) copy-start(f32[128]{0:T(128)S(1)} %fusion.57) | copy-start | bytes 1540
  186.7 4.6 %copy-start.10 = (f32[1024,768]{1,0:T(8,128)}, f32[1024,768]{1,0:T(8,128)S(1)}, u32[]{:S(2)}) copy-start(f32[1024,768]{1,0:T(8,128)S(1)} %fusion.21) | copy-start | bytes 9437188
  191.2 0.9 copy-start.21
  195.9 146.0 %all-gather.11.cloned.1.call-start = ((), (), s32[]{:S(2)}) async-start(), calls=%async_computation.6 | async-start | bytes 2359296 | tf_op jit(solution)/shard_map/all_gather | solution.py:367
  196.0 5.1 %copy-start.11 = (bf16[2,8,2,32,1152]{4,3,2,1,0:T(8,128)(2,1)S(1)}, bf16[2,8,2,32,1152]{4,3,2,1,0:T(8,128)(2,1)}, u32[]{:S(2)}) copy-start(bf16[2,8,2,32,1152]{4,3,2,1,0:T(8,128)(2,1)} %copy.108) | copy-start | bytes 7077892
  201.0 1.9 copy-start.44
  201.1 1.9 copy-start.46
  202.9 41.6 %copy-start.39 = (f32[128]{0:T(128)S(1)}, f32[128]{0:T(128)}, u32[]{:S(2)}) copy-start(f32[128]{0:T(128)} %copy-done.38) | copy-start | bytes 1540
  202.9 41.6 %copy-start.41 = (f32[128]{0:T(128)S(1)}, f32[128]{0:T(128)}, u32[]{:S(2)}) copy-start(f32[128]{0:T(128)} %copy-done.40) | copy-start | bytes 1540
  203.0 42.4 %copy-start.43 = (f32[128]{0:T(128)S(1)}, f32[128]{0:T(128)}, u32[]{:S(2)}) copy-start(f32[128]{0:T(128)} %copy-done.42) | copy-start | bytes 1540
  252.6 2.7 copy-start.8
  254.5 0.8 copy-start.4
  254.5 2.9 copy-start.17
  256.2 88.4 %reduce-scatter.5.cloned.1.call-start = ((), (), s32[]{:S(2)}) async-start(), calls=%async_computation.7 | async-start | bytes 2949120 | tf_op jit(solution)/shard_map/reduce_scatter | solution.py:355
  259.7 4.2 %copy-start.3 = (bf16[8,128,1024]{2,1,0:T(8,128)(2,1)S(1)}, bf16[8,128,1024]{2,1,0:T(8,128)(2,1)}, u32[]{:S(2)}) copy-start(bf16[8,128,1024]{2,1,0:T(8,128)(2,1)} %shard_map.146) | copy-start | bytes 6291460
  266.5 3.3 copy-start.16
  266.5 3.3 copy-start.45
  266.5 3.6 copy-start.47
  272.2 1.7 copy-start.37
  273.9 1.6 copy-start.2
  273.9 1.6 copy-start.14
  276.4 17.2 %copy-start.36 = (f32[2,1024]{1,0:T(2,128)S(1)}, f32[2,1024]{1,0:T(2,128)}, u32[]{:S(2)}) copy-start(f32[2,1024]{1,0:T(2,128)} %copy-done.35) | copy-start | bytes 24580
  293.5 13.4 %slice-start = ((s8[8388608]{0:T(1024)(128)(4,1)}), s8[4194304]{0:T(1024)(128)(4,1)S(1)}, s32[]{:S(2)}) async-start(s8[8388608]{0:T(1024)(128)(4,1)} %bitcast.180), calls=%async_computation.8 | async-start | bytes 8388608
  298.5 5.1 %copy-start.26 = (bf16[1024,2,32]{0,2,1:T(8,128)(2,1)S(1)}, bf16[1024,2,32]{0,2,1:T(8,128)(2,1)}, u32[]{:S(2)}) copy-start(bf16[1024,2,32]{0,2,1:T(8,128)(2,1)} %get-tuple-element.51) | copy-start | bytes 393220
  298.5 5.1 %copy-start.27 = (bf16[1024,2,32]{0,2,1:T(8,128)(2,1)S(1)}, bf16[1024,2,32]{0,2,1:T(8,128)(2,1)}, u32[]{:S(2)}) copy-start(bf16[1024,2,32]{0,2,1:T(8,128)(2,1)} %get-tuple-element.52) | copy-start | bytes 393220
  298.5 8.5 %slice-start.1 = ((s8[8388608]{0:T(1024)(128)(4,1)}), s8[4194304]{0:T(1024)(128)(4,1)S(1)}, s32[]{:S(2)}) async-start(s8[8388608]{0:T(1024)(128)(4,1)} %bitcast.180), calls=%async_computation.9 | async-start | bytes 8388608
  303.6 0.9 copy-start.7
  304.5 0.9 copy-start.24
  304.5 1.0 copy-start.25
  307.0 1.4 copy-start.13
  308.4 1.3 copy-start.34
  335.2 1.6 copy-start.15
  339.4 1.1 copy-start.5
  339.4 1.4 copy-start.9
  339.4 1.6 copy-start.20
  340.5 1.4 copy-start.19
  374.3 12.3 %copy-start.22 = (bf16[8,32,1152]{2,1,0:T(8,128)(2,1)S(1)}, bf16[8,32,1152]{2,1,0:T(8,128)(2,1)}, u32[]{:S(2)}) copy-start(bf16[8,32,1152]{2,1,0:T(8,128)(2,1)} %get-tuple-element.25) | copy-start | bytes 1769476
  376.5 10.1 %copy-start.31 = (bf16[4,32,1024]{2,1,0:T(8,128)(2,1)S(1)}, bf16[4,32,1024]{2,1,0:T(8,128)(2,1)}, u32[]{:S(2)}) copy-start(bf16[4,32,1024]{2,1,0:T(8,128)(2,1)} %get-tuple-element.24) | copy-start | bytes 786436
  384.7 3.5 copy-start.28
  386.7 6.2 %collective-permute-start = (bf16[32,1024]{1,0:T(8,128)(2,1)S(1)}, bf16[32,1024]{1,0:T(8,128)(2,1)S(1)}, u32[]{:S(2)}, u32[]{:S(2)}) collective-permute-start(bf16[32,1024]{1,0:T(8,128)(2,1)S(1)} %reduce_sum.207), channel_id=1, source_target_pairs={{0,0},{1,1},{2,4},{3,5},{4,8},{5,9},{6,12},{7,13},{8,16},{9,17},{1... | collective-permute-start | bytes 196616 | tf_op jit(solution)/shard_map/ppermute | solution.py:409
Sparse Core Ops, SparseCore 0:
  35.7 48.9 all-gather.6
  87.7 57.1 all-gather.4
  147.1 43.3 all-gather.8
  196.0 56.5 reduce-scatter.2
  256.3 38.8 all-gather.10
  298.1 35.7 reduce-scatter.4

commit v3 on v2

--- a/solution.py
+++ b/solution.py
@@ -294,9 +294,6 @@
         ],
         2,
     )
-    mlp_full = in_order(
-        lax.all_gather(mlp_cut.reshape(n_u * part, -1), ("dp", "blk"), axis=0, tiled=True)
-    )
     out_full = lax.all_gather(
         attention_output_weight, ("dp", "ulysses", "blk"), axis=0, tiled=True
     )
@@ -304,8 +301,6 @@
     qkv_w = first_full[:, :head_cols]
     gain_attn_f = first_full[:, head_cols].astype(f32)
     gain_mlp_f = first_full[:, head_cols + 1].astype(f32)
-    in_w = mlp_full[:, : 2 * ff_pad]
-    down_w = mlp_full[:, 2 * ff_pad :]
 
     inputs = inputs_low.astype(f32)
     tokens_all = tokens_all.reshape(length, width)
@@ -334,8 +329,17 @@
 
     middle = inputs + jnp.dot(back, out_full, preferred_element_type=f32)
     normed_mlp_own = layer_norm(middle, gain_mlp_f).astype(BF)
-    (normed_mlp,) = together([("line", normed_mlp_own, None)], 6)
+    normed_mlp, mlp_full = together(
+        [
+            ("line", normed_mlp_own, None),
+            ("copy", mlp_cut.reshape(n_u * part, -1), ("dp", "blk")),
+        ],
+        6,
+    )
     normed_mlp = normed_mlp.reshape(length, width)
+    mlp_full = in_order(mlp_full)
+    in_w = mlp_full[:, : 2 * ff_pad]
+    down_w = mlp_full[:, 2 * ff_pad :]
     hidden = jnp.dot(normed_mlp, in_w, preferred_element_type=f32)
 
     def gated(hidden):

time: 407 us -> 360 us (0.88)
  waiting for transfers between devices: 49.1 us -> 9.67 us
  matrix products: 49.9 us -> 44.5 us
    all_gather x1, waiting for transfers between devices: 41.6 us -> 0.02 us  [body(): lax.all_gather(attention_output_weight, ('dp', 'ulysses', 'blk'), axis=0,...]
    pallas_call x2, Pallas kernels: 67 us -> 61 us  [scatter_line(): pl.pallas_call(kernel, out_shape=jax.ShapeDtypeStruct((rows, cols), jnp.f...]
    unnamed x103 -> x113, local copies, waits for them, and re-layouts: 6.39 us -> 8.52 us
  transfers between devices with their start and end apart: 7 -> 6, of which waited for: 2 -> 1; matrix products, arithmetic and copies ran while one was open for 24% -> 28% of each run, Pallas kernels for 39% -> 50%
where the time goes in v3:
time: 360 us; the launch traced here: 353 us
  Pallas kernels  213 us (59%)
  matrix products  44.5 us (12%)
  local copies, waits for them, and re-layouts  37 us (10%)
  other arithmetic  32.2 us (9%)
  between operations  15.2 us (4%)
  waiting for transfers between devices  9.67 us (3%)
    pallas_call x7, Pallas kernels, together(): pl.pallas_call(kernel, out_shape=shapes, in_specs=[pl.BlockSpec(memory_sp...  152 us
    pallas_call x2, Pallas kernels, scatter_line(): pl.pallas_call(kernel, out_shape=jax.ShapeDtypeStruct((rows, cols), jnp.f...  61 us
    dot_general x4, matrix products, contract_rows(): lax.dot_general(left_side, right_side, (((0,), (0,)), ((), ())), preferre...  10 us
    reduce_scatter x1, waiting for transfers between devices, body(): lax.psum_scatter(mlp_part, 'ulysses', scatter_dimension=0, tiled=True)  8.87 us
    unnamed x113, local copies, waits for them, and re-layouts  8.52 us
  transfers between devices with their start and end apart: 6, of which 1 were waited for; matrix products, arithmetic and copies ran while one was open for 28% of the time, Pallas kernels for 50%

profile of v3, /device:TPU:0, one launch (start us, length us, event | category | flops | bytes accessed | tf_op | source)
XLA Modules:
  0.0 353.2 jit_solution(13124646506812571784)
XLA Ops:
  8.7 0.9 copy.114
  9.7 1.2 reshape.313
  10.9 1.7 reshape.311
  14.4 0.8 pad_maximum_fusion.1.refs_0_
  15.2 0.9 pad_maximum_fusion.refs_2_
  16.1 22.5 %shard_map.143 = (bf16[2,2,64,1024]{3,2,1,0:T(8,128)(2,1)}, bf16[8,32,512]{2,1,0:T(8,128)(2,1)}, bf16[8,32,1152]{2,1,0:T(8,128)(2,1)}) custom-call(bf16[2,2,64,1024]{3,2,1,0:T(8,128)(2,1)} %pad_maximum_fusion.1.refs_0_, bf16[8,32,512]{2,1,0:T(8,128)(2,1)} %pad_maximum_fusion.2.refs_1_, bf16[8,32,1152]{2,1,0:T(8,128)(2,1)} %pad_maximum_fusion.refs_2_), custom_call_target="tpu_custom_call" | custom-call | tf_op jit(solution)/shard_map/pallas_call | solution.py:161
  38.6 1.9 fusion.72
  41.3 29.2 %shard_map.144 = (bf16[4,256,512]{2,1,0:T(8,128)(2,1)}, bf16[8,128,1024]{2,1,0:T(8,128)(2,1)}) custom-call(bf16[256,512]{1,0:T(8,128)(2,1)} %bitcast.217, bf16[128,1024]{1,0:T(8,128)(2,1)} %bitcast.177), custom_call_target="tpu_custom_call" | custom-call | tf_op jit(solution)/shard_map/pallas_call | solution.py:161
  70.5 1.4 copy.81
  74.5 1.0 convolution_convert_fusion.6
  76.5 4.9 %fusion.73 = (f32[2,1024]{1,0:T(2,128)S(1)}, f32[2,1024,1024]{1,2,0:T(8,128)}) fusion(bf16[1024,2,32]{0,2,1:T(8,128)(2,1)S(1)} %get-tuple-element.55, bf16[1024,2,32]{0,2,1:T(8,128)(2,1)S(1)} %get-tuple-element.56, bf16[1024,2,32]{0,2,1:T(8,128)(2,1)S(1)} %get-tuple-element.45, bf16[1024,2,32]{0,2,1:T(8,128)(2,1)S(1)} %get-tuple-element.44), kind=kOutput, calls=%fused_computation.153 | convolution fusion | flops 275776512 | bytes 8921088 | tf_op jit(solution)/shard_map/sub | solution.py:320
  82.0 4.4 %fusion.31 = bf16[2,64,1024]{2,1,0:T(8,128)(2,1)S(1)} fusion(bf16[1024,2,192]{0,2,1:T(8,128)(2,1)} %bitcast.215, f32[2,1024,1024]{1,2,0:T(8,128)} %get-tuple-element.66, f32[2,1024]{1,0:T(2,128)S(1)} %get-tuple-element.65), kind=kOutput, calls=%fused_computation.58 | convolution fusion | flops 272760832 | bytes 8921088 | tf_op jit(solution)/shard_map/hqk,hke->qhe/dot_general | solution.py:325
  87.1 0.9 copy.83.refs_0_
  88.0 16.2 %shard_map.145 = bf16[8,128,128]{2,1,0:T(8,128)(2,1)} custom-call(bf16[8,128,128]{2,1,0:T(8,128)(2,1)} %copy.83.refs_0_), custom_call_target="tpu_custom_call" | custom-call | tf_op jit(solution)/shard_map/pallas_call | solution.py:161
  104.2 1.1 copy.84
  105.4 2.1 fusion.74
  107.8 0.8 multiply_convert_fusion.3.refs_0_
  108.6 31.9 %shard_map.146 = (bf16[8,128,1024]{2,1,0:T(8,128)(2,1)}, bf16[4,256,1152]{2,1,0:T(8,128)(2,1)}) custom-call(bf16[128,1024]{1,0:T(8,128)(2,1)} %multiply_convert_fusion.3.refs_0_, bf16[256,1152]{1,0:T(8,128)(2,1)} %bitcast.211), custom_call_target="tpu_custom_call" | custom-call | tf_op jit(solution)/shard_map/pallas_call | solution.py:161
  140.5 2.1 copy.85
  142.8 1.8 fusion.21
  144.6 4.4 %multiply_convert_fusion.2 = (bf16[1024,384]{1,0:T(8,128)(2,1)S(1)}, f32[1024,384]{1,0:T(8,128)}) fusion(f32[1024,768]{1,0:T(8,128)S(1)} %fusion.21), kind=kLoop, calls=%fused_computation.29 | loop fusion | flops 25952256 | bytes 5505024 | tf_op jit(solution)/shard_map/convert_element_type | solution.py:349
  149.0 0.9 copy-done.23
  149.9 2.6 convolution_convert_fusion.1
  152.8 5.1 %fusion.49 = (f32[1024,384]{1,0:T(8,128)S(1)}, f32[1024,384]{1,0:T(8,128)S(1)}) fusion(f32[1024,384]{1,0:T(8,128)} %get-tuple-element.39, f32[1024,768]{1,0:T(8,128)} %copy-done.9, bf16[1024,1024]{1,0:T(8,128)(2,1)} %all-gather.6.cloned.1.call-done, bf16[1024,1152]{1,0:T(8,128)(2,1)} %bitcast.186), kind=kOutput, calls=%fused_computation.94 | convolution fusion | flops 811597824 | bytes 10747904 | tf_op jit(solution)/shard_map/dot_general | solution.py:350
  157.9 1.8 convolution_convert_fusion.2
  159.8 35.8 %shard_map.147 = f32[128,1024]{1,0:T(8,128)S(1)} custom-call(bf16[8,128,1024]{2,1,0:T(8,128)(2,1)S(1)} %bitcast.174), custom_call_target="tpu_custom_call" | custom-call | tf_op jit(solution)/shard_map/pallas_call | solution.py:224
  195.6 0.8 multiply_reduce_fusion.3
  196.9 8.9 %reduce-scatter.3.cloned.1.call-done = bf16[128,1024]{1,0:T(8,128)(2,1)} async-done(((bf16[1024,1024]{1,0:T(8,128)(2,1)}), bf16[128,1024]{1,0:T(8,128)(2,1)}) %reduce-scatter.3.cloned.1.call-update) | async-done | bytes 262160 | tf_op jit(solution)/shard_map/reduce_scatter | solution.py:355
  205.8 1.9 fusion.71
  207.7 0.8 copy-done.3
  208.5 0.8 fusion.50
  209.4 1.1 convert_reduce_fusion.1
  210.9 2.0 multiply_convert_fusion.1
  212.9 4.1 %copy.92 = bf16[1024,1024]{1,0:T(8,128)(2,1)} copy(bf16[1024,1024]{0,1:T(8,128)(2,1)} %bitcast.179) | data formatting | bytes 4194304 | tf_op jit(solution)/shard_map/dot_general | solution.py:54
  217.0 2.6 copy.96
  219.6 3.1 convolution_convert_fusion.4
  223.1 1.8 convolution_convert_fusion.3
  225.2 1.7 copy.97
  226.9 1.6 copy-done.2
  228.4 0.8 convolution_convert_fusion.8
  229.5 0.9 copy.87
  230.3 14.8 %shard_map.148 = bf16[8,128,128]{2,1,0:T(8,128)(2,1)} custom-call(bf16[8,128,128]{2,1,0:T(8,128)(2,1)} %bitcast.205), custom_call_target="tpu_custom_call" | custom-call | tf_op jit(solution)/shard_map/pallas_call | solution.py:161
  245.1 1.1 copy.88
  246.4 4.9 %multiply_reduce_fusion = (f32[2,1024]{1,0:T(2,128)S(1)}, f32[2,1024,1024]{1,2,0:T(8,128)S(1)}) fusion(f32[2,1024,1024]{1,2,0:T(8,128)} %get-tuple-element.66, f32[2,1024]{1,0:T(2,128)S(1)} %copy-done.41, bf16[1024,2,192]{0,2,1:T(8,128)(2,1)} %bitcast.216, bf16[1024,2,64]{0,2,1:T(8,128)(2,1)S(1)} %reshape.326), kind=kOutput, calls=%fused_computation.2 | convolution fusion | flops 274724864 | bytes 17317888 | tf_op jit(solution)/shard_map/hqe,hke->hqk/dot_general | solution.py:376
  251.4 5.0 %multiply_convert_fusion = bf16[2,1024,1024]{1,2,0:T(8,128)(2,1)S(1)} fusion(f32[2,1024,1024]{1,2,0:T(8,128)S(1)} %get-tuple-element.70, f32[2,1024]{1,0:T(2,128)S(1)} %get-tuple-element.69, f32[2,1024,1024]{1,2,0:T(8,128)} %get-tuple-element.66, f32[2,1024]{1,0:T(2,128)S(1)} %copy-done.41), kind=kLoop, calls=%fused_computation.1 | loop fusion | flops 8388608 | bytes 20987904 | tf_op jit(solution)/shard_map/convert_element_type | solution.py:378
  256.5 0.8 fusion.30
  257.5 0.8 copy-done.27
  258.3 1.4 fusion.29
  259.9 1.4 fusion.26
  261.3 1.3 convolution_convert_fusion
  262.6 25.2 %shard_map.149 = f32[128,1024]{1,0:T(8,128)S(1)} custom-call(bf16[8,128,1024]{2,1,0:T(8,128)(2,1)S(1)} %bitcast.175), custom_call_target="tpu_custom_call" | custom-call | tf_op jit(solution)/shard_map/pallas_call | solution.py:224
  289.4 2.4 convolution_convert_fusion.5
  292.0 1.1 copy.95
  293.6 0.8 maximum_bitcast_fusion.2.refs_0_
  294.5 2.7 convolution_convert_fusion.7
  297.2 29.7 %shard_map.150 = (bf16[2,2,64,1024]{3,2,1,0:T(8,128)(2,1)}, bf16[4,256,512]{2,1,0:T(8,128)(2,1)}, bf16[4,32,1024]{2,1,0:T(8,128)(2,1)}, bf16[8,32,1152]{2,1,0:T(8,128)(2,1)}) custom-call(bf16[2,2,64,1024]{3,2,1,0:T(8,128)(2,1)} %maximum_bitcast_fusion.2.refs_0_, bf16[4,256,512]{2,1,0:T(8,128)(2,1)} %bitcast.182, bf16[4,32,1024]{2,1,0:T(8,128)(2,1)} %bitcast.196, ...), custom_call_target="tpu_custom_call" | custom-call | tf_op jit(solution)/shard_map/pallas_call | solution.py:161
  327.0 2.2 reduce_sum.205
  329.2 8.2 %shard_map.151 = bf16[8,32,512]{2,1,0:T(8,128)(2,1)} custom-call(bf16[8,32,512]{2,1,0:T(8,128)(2,1)} %bitcast.199), custom_call_target="tpu_custom_call" | custom-call | tf_op jit(solution)/shard_map/pallas_call | solution.py:161
  337.3 0.9 convert_reduce_fusion.4
  338.3 1.0 convert_bitcast_fusion.2
  340.0 0.8 copy.111
  340.8 0.9 bitcast_convert_fusion
  342.1 0.9 reshape.339
  343.7 1.2 reshape.338
  (181 shorter events, 17.3 us)
Async XLA Ops:
  7.2 98.2 %all-gather.4.cloned.1.call-start = ((), (), s32[]{:S(2)}) async-start(), calls=%async_computation.2 | async-start | bytes 2162688 | tf_op jit(solution)/shard_map/all_gather | solution.py:297
  7.9 144.9 %all-gather.6.cloned.1.call-start = ((), (), s32[]{:S(2)}) async-start(), calls=%async_computation.4 | async-start | bytes 2359296 | tf_op jit(solution)/shard_map/all_gather | solution.py:307
  12.6 1.8 copy-start.37
  12.6 1.8 copy-start.38
  40.5 165.3 %reduce-scatter.3.cloned.1.call-start = ((), (), s32[]{:S(2)}) async-start(), calls=%async_computation.3 | async-start | bytes 2359296 | tf_op jit(solution)/shard_map/reduce_scatter | solution.py:355
  41.3 34.4 %copy-start.5 = (f32[1024,32]{0,1:T(8,128)}, f32[1024,32]{0,1:T(8,128)S(1)}, u32[]{:S(2)}) copy-start(f32[1024,32]{0,1:T(8,128)S(1)} %get-tuple-element.64) | copy-start | bytes 393220
  70.5 1.9 copy-start
  72.0 2.5 copy-start.12
  75.5 0.9 copy-start.35
  76.5 4.9 %copy-start.26 = (bf16[1024,2,32]{0,2,1:T(8,128)(2,1)}, bf16[1024,2,32]{0,2,1:T(8,128)(2,1)S(1)}, u32[]{:S(2)}) copy-start(bf16[1024,2,32]{0,2,1:T(8,128)(2,1)S(1)} %get-tuple-element.44) | copy-start | bytes 393220
  76.5 4.9 %copy-start.28 = (bf16[1024,2,32]{0,2,1:T(8,128)(2,1)}, bf16[1024,2,32]{0,2,1:T(8,128)(2,1)S(1)}, u32[]{:S(2)}) copy-start(bf16[1024,2,32]{0,2,1:T(8,128)(2,1)S(1)} %get-tuple-element.45) | copy-start | bytes 393220
  76.5 4.9 %copy-start.30 = (bf16[1024,2,32]{0,2,1:T(8,128)(2,1)}, bf16[1024,2,32]{0,2,1:T(8,128)(2,1)S(1)}, u32[]{:S(2)}) copy-start(bf16[1024,2,32]{0,2,1:T(8,128)(2,1)S(1)} %get-tuple-element.55) | copy-start | bytes 393220
  76.5 4.9 %copy-start.32 = (bf16[1024,2,32]{0,2,1:T(8,128)(2,1)}, bf16[1024,2,32]{0,2,1:T(8,128)(2,1)S(1)}, u32[]{:S(2)}) copy-start(bf16[1024,2,32]{0,2,1:T(8,128)(2,1)S(1)} %get-tuple-element.56) | copy-start | bytes 393220
  81.4 0.6 copy-start.40
  86.4 0.7 copy-start.20
  86.4 19.0 %copy-start.1 = (bf16[2,1,64,1024]{3,2,1,0:T(8,128)(2,1)S(1)}, bf16[2,1,64,1024]{3,2,1,0:T(8,128)(2,1)}, u32[]{:S(2)}) copy-start(bf16[2,1,64,1024]{3,2,1,0:T(8,128)(2,1)} %get-tuple-element.54) | copy-start | bytes 786436
  107.5 35.1 %copy-start.43 = (f32[128]{0:T(128)}, f32[128]{0:T(128)S(1)}, u32[]{:S(2)}) copy-start(f32[128]{0:T(128)S(1)} %broadcast_multiply_fusion.2) | copy-start | bytes 1540
  107.7 34.9 %copy-start.47 = (f32[128]{0:T(128)}, f32[128]{0:T(128)S(1)}, u32[]{:S(2)}) copy-start(f32[128]{0:T(128)S(1)} %multiply_reduce_fusion.5) | copy-start | bytes 1540
  107.7 34.8 %copy-start.45 = (f32[128]{0:T(128)}, f32[128]{0:T(128)S(1)}, u32[]{:S(2)}) copy-start(f32[128]{0:T(128)S(1)} %fusion.57) | copy-start | bytes 1540
  140.5 2.3 copy-start.16
  142.6 6.4 %copy-start.10 = (bf16[2,2,8,32,1152]{4,3,1,2,0:T(8,128)(2,1)}, bf16[2,2,8,32,1152]{4,3,1,2,0:T(8,128)(2,1)S(1)}, u32[]{:S(2)}) copy-start(bf16[2,2,8,32,1152]{4,3,1,2,0:T(8,128)(2,1)S(1)} %copy.85) | copy-start | bytes 7077892
  144.6 4.4 %copy-start.9 = (f32[1024,768]{1,0:T(8,128)}, f32[1024,768]{1,0:T(8,128)S(1)}, u32[]{:S(2)}) copy-start(f32[1024,768]{1,0:T(8,128)S(1)} %fusion.21) | copy-start | bytes 9437188
  149.0 0.9 copy-start.23
  152.5 142.0 %all-gather.8.cloned.1.call-start = ((), (), s32[]{:S(2)}) async-start(), calls=%async_computation.5 | async-start | bytes 2359296 | tf_op jit(solution)/shard_map/all_gather | solution.py:371
  152.8 5.1 %copy-start.11 = (bf16[2,2,8,32,1152]{4,3,1,2,0:T(8,128)(2,1)S(1)}, bf16[2,2,8,32,1152]{4,3,1,2,0:T(8,128)(2,1)}, u32[]{:S(2)}) copy-start(bf16[2,2,8,32,1152]{4,3,1,2,0:T(8,128)(2,1)} %copy-done.10) | copy-start | bytes 7077892
  157.9 1.9 copy-start.49
  157.9 1.9 copy-start.51
  159.7 35.9 %copy-start.44 = (f32[128]{0:T(128)S(1)}, f32[128]{0:T(128)}, u32[]{:S(2)}) copy-start(f32[128]{0:T(128)} %copy-done.43) | copy-start | bytes 1540
  159.8 35.9 %copy-start.46 = (f32[128]{0:T(128)S(1)}, f32[128]{0:T(128)}, u32[]{:S(2)}) copy-start(f32[128]{0:T(128)} %copy-done.45) | copy-start | bytes 1540
  159.8 36.6 %copy-start.48 = (f32[128]{0:T(128)S(1)}, f32[128]{0:T(128)}, u32[]{:S(2)}) copy-start(f32[128]{0:T(128)} %copy-done.47) | copy-start | bytes 1540
  205.8 2.7 copy-start.7
  207.7 0.8 copy-start.3
  207.7 2.9 copy-start.19
  209.4 87.8 %reduce-scatter.5.cloned.1.call-start = ((), (), s32[]{:S(2)}) async-start(), calls=%async_computation.6 | async-start | bytes 2949120 | tf_op jit(solution)/shard_map/reduce_scatter | solution.py:359
  212.9 4.1 %copy-start.17 = (bf16[8,128,1024]{2,1,0:T(8,128)(2,1)S(1)}, bf16[8,128,1024]{2,1,0:T(8,128)(2,1)}, u32[]{:S(2)}) copy-start(bf16[8,128,1024]{2,1,0:T(8,128)(2,1)} %get-tuple-element.24) | copy-start | bytes 6291460
  217.0 2.6 copy-start.24
  219.6 3.1 copy-start.18
  219.6 3.1 copy-start.50
  219.6 3.5 copy-start.52
  225.1 1.7 copy-start.42
  226.8 1.6 copy-start.2
  226.8 1.6 copy-start.14
  229.3 17.1 %copy-start.41 = (f32[2,1024]{1,0:T(2,128)S(1)}, f32[2,1024]{1,0:T(2,128)}, u32[]{:S(2)}) copy-start(f32[2,1024]{1,0:T(2,128)} %copy-done.40) | copy-start | bytes 24580
  246.4 13.4 %slice-start = ((s8[8388608]{0:T(1024)(128)(4,1)}), s8[4194304]{0:T(1024)(128)(4,1)S(1)}, s32[]{:S(2)}) async-start(s8[8388608]{0:T(1024)(128)(4,1)} %bitcast.180), calls=%async_computation.7 | async-start | bytes 8388608
  251.4 5.1 %copy-start.31 = (bf16[1024,2,32]{0,2,1:T(8,128)(2,1)S(1)}, bf16[1024,2,32]{0,2,1:T(8,128)(2,1)}, u32[]{:S(2)}) copy-start(bf16[1024,2,32]{0,2,1:T(8,128)(2,1)} %copy-done.30) | copy-start | bytes 393220
  251.4 5.1 %copy-start.33 = (bf16[1024,2,32]{0,2,1:T(8,128)(2,1)S(1)}, bf16[1024,2,32]{0,2,1:T(8,128)(2,1)}, u32[]{:S(2)}) copy-start(bf16[1024,2,32]{0,2,1:T(8,128)(2,1)} %copy-done.32) | copy-start | bytes 393220
  251.4 8.5 %slice-start.1 = ((s8[8388608]{0:T(1024)(128)(4,1)}), s8[4194304]{0:T(1024)(128)(4,1)S(1)}, s32[]{:S(2)}) async-start(s8[8388608]{0:T(1024)(128)(4,1)} %bitcast.180), calls=%async_computation.8 | async-start | bytes 8388608
  256.5 0.9 copy-start.6
  257.4 0.9 copy-start.27
  257.4 1.0 copy-start.29
  259.9 1.4 copy-start.13
  261.3 1.3 copy-start.39
  287.8 1.6 copy-start.15
  291.9 1.1 copy-start.4
  292.0 1.4 copy-start.8
  292.0 1.6 copy-start.22
  293.0 1.4 copy-start.21
  326.9 12.3 %copy-start.25 = (bf16[8,32,1152]{2,1,0:T(8,128)(2,1)S(1)}, bf16[8,32,1152]{2,1,0:T(8,128)(2,1)}, u32[]{:S(2)}) copy-start(bf16[8,32,1152]{2,1,0:T(8,128)(2,1)} %get-tuple-element.29) | copy-start | bytes 1769476
  329.2 10.1 %copy-start.36 = (bf16[4,32,1024]{2,1,0:T(8,128)(2,1)S(1)}, bf16[4,32,1024]{2,1,0:T(8,128)(2,1)}, u32[]{:S(2)}) copy-start(bf16[4,32,1024]{2,1,0:T(8,128)(2,1)} %get-tuple-element.28) | copy-start | bytes 786436
  337.3 3.5 copy-start.34
  339.4 6.2 %collective-permute-start = (bf16[32,1024]{1,0:T(8,128)(2,1)S(1)}, bf16[32,1024]{1,0:T(8,128)(2,1)S(1)}, u32[]{:S(2)}, u32[]{:S(2)}) collective-permute-start(bf16[32,1024]{1,0:T(8,128)(2,1)S(1)} %reduce_sum.207), channel_id=1, source_target_pairs={{0,0},{1,1},{2,4},{3,5},{4,8},{5,9},{6,12},{7,13},{8,16},{9,17},{1... | collective-permute-start | bytes 196616 | tf_op jit(solution)/shard_map/ppermute | solution.py:413
Sparse Core Ops, SparseCore 0:
  10.9 77.9 all-gather.3
  91.1 44.1 all-gather.5
  152.6 53.1 reduce-scatter.2
  209.5 38.8 all-gather.7
  251.3 35.7 reduce-scatter.4
